TPU v7x, 32 devices: a whole 2x2x4 slice. The times are simulated.
32 devices in a mesh: dp: 4 (over y, core), fsdp: 8 (over z, x).
Axes of the slice: x: 2, y: 2, z: 4, core: 2. Of those that a mesh axis runs over, the one named last changes fastest.
Arguments:
- features: bfloat16 [1536, 49, 2048], P(('dp', 'fsdp')), may hold values from -15 to 15
- view_order: int32 [32, 48], P(('dp', 'fsdp')), may hold values from 0 to 47, each once within a row
- conv_one: float32 [2048, 512], P('fsdp', 'dp'), may hold values from -0.125 to 0.125
- conv_two: float32 [4608, 512], P('fsdp', 'dp'), may hold values from -0.09375 to 0.09375
- conv_three: float32 [512, 2048], P('fsdp', 'dp'), may hold values from -0.25 to 0.25
- proj_one: float32 [2048, 1024], P('fsdp', 'dp'), may hold values from -0.125 to 0.125
- proj_two: float32 [1024, 128], P('fsdp', 'dp'), may hold values from -0.1875 to 0.1875
- norm_params: float32 [2, 4096], P(None, ('dp', 'fsdp')), may hold values from -2 to 3, as said below
- first_conv_one: float32 [2048, 512], P('fsdp', 'dp'), may hold values from -6.1035156e-05 to 6.1035156e-05
- first_conv_two: float32 [4608, 512], P('fsdp', 'dp'), may hold values from -6.1035156e-05 to 6.1035156e-05
- first_conv_three: float32 [512, 2048], P('fsdp', 'dp'), may hold values from -6.1035156e-05 to 6.1035156e-05
- first_proj_one: float32 [2048, 1024], P('fsdp', 'dp'), may hold values from -6.1035156e-05 to 6.1035156e-05
- first_proj_two: float32 [1024, 128], P('fsdp', 'dp'), may hold values from -6.1035156e-05 to 6.1035156e-05
- first_norm: float32 [2, 4096], P(None, ('dp', 'fsdp')), may hold values from -6.1035156e-05 to 6.1035156e-05
- second_conv_one: float32 [2048, 512], P('fsdp', 'dp'), may hold values from 7.4706436e-13 to 1.195303e-11
- second_conv_two: float32 [4608, 512], P('fsdp', 'dp'), may hold values from 7.4706436e-13 to 1.195303e-11
- second_conv_three: float32 [512, 2048], P('fsdp', 'dp'), may hold values from 7.4706436e-13 to 1.195303e-11
- second_proj_one: float32 [2048, 1024], P('fsdp', 'dp'), may hold values from 7.4706436e-13 to 1.195303e-11
- second_proj_two: float32 [1024, 128], P('fsdp', 'dp'), may hold values from 7.4706436e-13 to 1.195303e-11
- second_norm: float32 [2, 4096], P(None, ('dp', 'fsdp')), may hold values from 7.4706436e-13 to 1.195303e-11
Outputs:
- loss: float32 [], replicated
- input_grad: float32 [1536, 49, 2048], P(('dp', 'fsdp'))
- grad_norm: float32 [], replicated
- new_conv_one: float32 [2048, 512], P('fsdp', 'dp')
- new_conv_two: float32 [4608, 512], P('fsdp', 'dp')
- new_conv_three: float32 [512, 2048], P('fsdp', 'dp')
- new_proj_one: float32 [2048, 1024], P('fsdp', 'dp')
- new_proj_two: float32 [1024, 128], P('fsdp', 'dp')
- new_norm: float32 [2, 4096], P(None, ('dp', 'fsdp'))
- new_first_conv_one: float32 [2048, 512], P('fsdp', 'dp')
- new_first_conv_two: float32 [4608, 512], P('fsdp', 'dp')
- new_first_conv_three: float32 [512, 2048], P('fsdp', 'dp')
- new_first_proj_one: float32 [2048, 1024], P('fsdp', 'dp')
- new_first_proj_two: float32 [1024, 128], P('fsdp', 'dp')
- new_first_norm: float32 [2, 4096], P(None, ('dp', 'fsdp'))
- new_second_conv_one: float32 [2048, 512], P('fsdp', 'dp')
- new_second_conv_two: float32 [4608, 512], P('fsdp', 'dp')
- new_second_conv_three: float32 [512, 2048], P('fsdp', 'dp')
- new_second_proj_one: float32 [2048, 1024], P('fsdp', 'dp')
- new_second_proj_two: float32 [1024, 128], P('fsdp', 'dp')
- new_second_norm: float32 [2, 4096], P(None, ('dp', 'fsdp'))
Inputs may be any that keep to these rules, and one draw needn't show every extreme that they name: `view_order`: in row d, entry j = 2 i + k says that slot j of that device's views holds view k of image d * 24 + i. `norm_params`: row 0 is positive.
All inputs are finite; a program needn't handle non-finite values.
Results may differ from a plain program's by a relative error of at most 0.039.
Values may be sent and summed in bfloat16 or wider, within the bound.
A program may use at most 384 MiB of HBM per device.

v0:
```python
from typing import Any, NamedTuple

import jax
import jax.numpy as jnp
from jax import lax
from jax.experimental import pallas as pl
from jax.experimental.pallas import tpu as pltpu
from jax.sharding import PartitionSpec as P

C_IN = 2048
C_MID = 512
P_HID = 1024
P_OUT = 128
SIDE = 7
STEP = 10
PIX = 49
LANES = 128
BLOCKS = C_IN // C_MID
CHUNKS = SIDE
SLOTS = 6


highest = lax.Precision.HIGHEST
bf16 = jnp.bfloat16
f32 = jnp.float32
norm_epsilon = 1e-05
ridge_term = 0.01
clip_level = 0.1
beta_first = 0.9
beta_second = 0.999
adam_epsilon = 1e-08
decay_rate = 0.05
norm_rate = 0.5
bell_scale = 0.3989422804014327
root_half = 0.5**0.5
bell_rate = -0.7213475204444817
DP, FSDP = "dp", "fsdp"


def gelu_pair(values):
    below = 0.5 + 0.5 * lax.erf(values * root_half)
    bell = jnp.exp2(values * values * bell_rate)
    return values * below, below + values * bell * bell_scale


def dot(left, right):
    return jnp.dot(left, right, preferred_element_type=f32)


def dot_cols(left, right):
    return lax.dot_general(left, right, (((1,), (1,)), ((), ())), preferred_element_type=f32)


def dot_rows(left, right):
    return lax.dot_general(left, right, (((0,), (0,)), ((), ())), preferred_element_type=f32)


def exact_cols(left, right):
    return lax.dot_general(
        left, right, (((1,), (1,)), ((), ())), precision=highest, preferred_element_type=f32
    )


def exact_rows(left, right):
    return lax.dot_general(
        left, right, (((0,), (0,)), ((), ())), precision=highest, preferred_element_type=f32
    )


def exact_dot(left, right):
    return jnp.dot(left, right, precision=highest, preferred_element_type=f32)


def inverse_factors(matrices):
    row_top = lax.broadcasted_iota(jnp.int32, (8, P_OUT), 0)
    row_all = lax.broadcasted_iota(jnp.int32, (P_OUT, P_OUT), 0)
    col_all = lax.broadcasted_iota(jnp.int32, (P_OUT, P_OUT), 1)

    def one_step(place, left, right):
        scale = lax.rsqrt(left[place : place + 1, place : place + 1])
        left_row = left[place : place + 1, :] * scale
        right_row = right[place : place + 1, :] * scale
        column = left[:, place : place + 1] * scale
        left = left - column * left_row
        right = right - column * right_row
        here = row_top == place
        left = jnp.concatenate([jnp.where(here, 0.0, left[:8]), left[8:]], axis=0)
        right = jnp.concatenate(
            [jnp.where(here, jnp.broadcast_to(right_row, (8, P_OUT)), right[:8]), right[8:]], axis=0
        )
        return left, right

    def panel(_, pairs):
        pairs = list(pairs)
        for place in range(8):
            for which in range(len(pairs)):
                pairs[which] = one_step(place, *pairs[which])
        return tuple(
            (
                pltpu.roll(jnp.concatenate([left[8:], left[:8]], axis=0), P_OUT - 8, 1),
                jnp.concatenate([right[8:], right[:8]], axis=0),
            )
            for left, right in pairs
        )

    start = tuple((matrix, (row_all == col_all).astype(f32)) for matrix in matrices)
    done = lax.fori_loop(0, P_OUT // 8, panel, start)
    return [right for _, right in done]


def pack_pair(first, second):
    row = lax.broadcasted_iota(jnp.int32, (P_OUT, P_OUT), 0)
    col = lax.broadcasted_iota(jnp.int32, (P_OUT, P_OUT), 1)
    packed = jnp.where(row >= col, first, second.T)
    diagonal = jnp.sum(jnp.where(row == col, second, 0.0), axis=0, keepdims=True)
    return packed, diagonal


def unpack_pair(packed, diagonal):
    row = lax.broadcasted_iota(jnp.int32, (P_OUT, P_OUT), 0)
    col = lax.broadcasted_iota(jnp.int32, (P_OUT, P_OUT), 1)
    turned = packed.T
    first = jnp.where(row >= col, packed, turned)
    second = jnp.where(row < col, packed, jnp.where(row == col, diagonal, turned))
    return first, second


class Ins(NamedTuple):
    features: Any
    order: Any
    norm: Any
    shards: Any


class Outs(NamedTuple):
    slope: Any
    features_grad: Any
    norm_grad: Any
    scalars: Any
    grads: Any


class SumRoom(NamedTuple):
    dp: Any
    fsdp: Any
    s0: Any
    r0: Any
    s1: Any
    r1: Any


class MatrixRoom(NamedTuple):
    pack: Any
    dp: Any
    fsdp: Any
    all: Any
    s0: Any
    r0: Any
    s1: Any
    r1: Any
    s2: Any
    r2: Any


class Mem(NamedTuple):
    w: Any
    g1: Any
    row_sums: Any
    r3: Any
    r4: Any
    r5: Any
    stage: Any
    stage_sem: Any
    column_sem: Any
    h1: Any
    d1: Any
    h2: Any
    d2: Any
    a2: Any
    h3: Any
    pad1: Any
    pad2: Any
    pool: Any
    pool_slope: Any
    pool_bend: Any
    pooled: Any
    proj_act: Any
    proj_slope: Any
    proj_hidden: Any
    coef: Any
    stats: Any
    norm: Any
    norm_tiles: Any
    norm_s0: Any
    norm_r0: Any
    norm_s1: Any
    norm_r1: Any
    bulk_send: Any
    bulk_recv: Any
    mats: Any
    sums: Any
    squares: Any


class Plan:
    def __init__(self, dp_size, fsdp_size, views, inside):
        self.dp = dp_size
        self.fsdp = fsdp_size
        self.devices = dp_size * fsdp_size
        self.views = views
        self.rows = views * PIX
        self.chunk = views * SIDE
        self.inside = inside
        self.z = 4
        self.x = 2
        self.half = (128, 288, 32, 128, 16)
        self.width = (128, 128, 512, 256, 128)
        piece = P_OUT + 8
        self.embed_rows = -(-piece // (8 * dp_size)) * 8


def kernel(plan, *refs):
    ins, outs, mem = Ins(*refs[:3], refs[3:8]), Outs(*refs[8:12], refs[12:17]), refs[17]
    views, chunk, rows = plan.views, plan.chunk, plan.rows
    row_total = float(rows * plan.devices)
    view_total = float(views * plan.devices)
    image_total = float(views * plan.devices // 2)
    dp_me, fsdp_me = lax.axis_index(DP), lax.axis_index(FSDP)
    y_me, c_me = dp_me // 2, dp_me % 2
    z_me, x_me = fsdp_me // 2, fsdp_me % 2
    y_other, c_other, x_other = 1 - y_me, 1 - c_me, 1 - x_me

    barrier = pltpu.get_barrier_semaphore()

    @pl.loop(1, plan.dp)
    def _(step):
        pl.semaphore_signal(
            barrier, 1, device_id={DP: lax.rem(dp_me + step, plan.dp)}, device_id_type=pl.DeviceIdType.MESH
        )

    @pl.loop(1, plan.fsdp)
    def _(step):
        pl.semaphore_signal(
            barrier, 1, device_id={FSDP: lax.rem(fsdp_me + step, plan.fsdp)}, device_id_type=pl.DeviceIdType.MESH
        )

    pl.semaphore_wait(barrier, plan.dp + plan.fsdp - 2)

    def share(axis, size, me, source_of, slots, send, recv):
        def outgoing(step):
            partner = lax.rem(me + step, size)
            return pltpu.make_async_remote_copy(
                src_ref=source_of(partner),
                dst_ref=slots.at[me],
                send_sem=send.at[step],
                recv_sem=recv.at[me],
                device_id={axis: partner},
                device_id_type=pl.DeviceIdType.MESH,
            )

        def incoming(step):
            source = lax.rem(me + step, size)
            return pltpu.make_async_remote_copy(
                src_ref=slots.at[source],
                dst_ref=slots.at[source],
                send_sem=send.at[step],
                recv_sem=recv.at[source],
                device_id={axis: source},
                device_id_type=pl.DeviceIdType.MESH,
            )

        def start():
            pl.loop(1, size)(lambda step: outgoing(step).start())

        def wait():
            pl.loop(1, size)(lambda step: incoming(step).wait_recv())
            pl.loop(1, size)(lambda step: outgoing(step).wait_send())

        return start, wait

    def add_slots(slots, size):
        total = slots[0]
        for place in range(1, size):
            total = total + slots[place]
        return total

    class Sum:
        def __init__(self, which):
            part = mem.sums[(0, 1, 2, 3, 4, 4, 5, 0, 1, 6)[which]]
            self.dp_slots, self.fsdp_slots = part.dp, part.fsdp
            self.dp_copy = share(
                DP, plan.dp, dp_me, lambda _: self.dp_slots.at[dp_me], self.dp_slots, part.s0, part.r0
            )
            self.fsdp_copy = share(
                FSDP, plan.fsdp, fsdp_me, lambda _: self.fsdp_slots.at[fsdp_me], self.fsdp_slots, part.s1, part.r1
            )

        def start(self, *values):
            for place, value in enumerate(values):
                self.dp_slots[dp_me, place : place + 1, :] = value
            self.dp_copy[0]()

        def middle(self):
            self.dp_copy[1]()
            self.fsdp_slots[fsdp_me] = add_slots(self.dp_slots, plan.dp)
            self.fsdp_copy[0]()

        def finish(self):
            self.fsdp_copy[1]()
            return add_slots(self.fsdp_slots, plan.fsdp)

        def all(self, *values):
            self.start(*values)
            self.middle()
            return self.finish()

    def sum_matrix(which, matrix, extra):
        part = mem.mats[which]
        size = plan.embed_rows
        pack = part.pack
        flat = jnp.concatenate(
            [matrix] + extra + [jnp.zeros((size * plan.dp - P_OUT - len(extra), P_OUT), f32)], axis=0
        )
        for place in range(plan.dp):
            pack[place] = flat[place * size : (place + 1) * size]
        start, wait = share(DP, plan.dp, dp_me, lambda to: pack.at[to], part.dp, part.s0, part.r0)
        start()
        part.dp[dp_me] = pack[dp_me]
        wait()
        part.fsdp[fsdp_me] = add_slots(part.dp, plan.dp)
        start, wait = share(
            FSDP, plan.fsdp, fsdp_me, lambda _: part.fsdp.at[fsdp_me], part.fsdp, part.s1, part.r1
        )
        start()
        wait()
        part.all[dp_me] = add_slots(part.fsdp, plan.fsdp)
        start, wait = share(
            DP, plan.dp, dp_me, lambda _: part.all.at[dp_me], part.all, part.s2, part.r2
        )
        start()
        wait()
        total = jnp.concatenate([part.all[place] for place in range(plan.dp)], axis=0)
        return total[:P_OUT], [total[P_OUT + place : P_OUT + place + 1] for place in range(len(extra))]

    weights = mem.w
    everything = slice(None)

    def row_span(which, half):
        if isinstance(half, tuple):
            return half
        size = plan.half[which]
        if half is None:
            return 0, 2 * size
        return half * size, size

    def column_span(which, dp_index):
        width = plan.width[which]
        return pl.ds(pl.multiple_of(dp_index * width, width), width)

    def places(which, z_index, x_index, dp_index, half, flat=True):
        start, size = row_span(which, half)
        if which == 1 and flat:
            z_list = range(plan.z) if z_index is None else [z_index]
            x_list = range(plan.x) if x_index is None else [x_index]
            return [
                (
                    pl.ds(pl.multiple_of((z_one * plan.x + x_one) * 576 + start, 16), size),
                    column_span(which, dp_index),
                )
                for z_one in z_list
                for x_one in x_list
            ]
        z_one = everything if z_index is None else z_index
        x_one = everything if x_index is None else x_index
        if which == 2:
            return [(dp_index, z_one, x_one, pl.ds(start, size), everything)]
        if which == 4:
            return [(z_one, x_one, pl.ds(pl.multiple_of(dp_index * 32 + start, 16), size), everything)]
        return [(z_one, x_one, pl.ds(start, size), column_span(which, dp_index))]

    recv_parts = {
        1: lambda index: mem.h3.at[index],
        0: lambda index: mem.r4.at[index],
        2: lambda index: mem.r3.at[index],
        3: lambda index: mem.r4.at[index],
        4: lambda index: mem.r5.at[index],
    }

    counter = [0]

    class Batch:
        def __init__(self, sources, targets, landings, axis, partner):
            base = counter[0]
            counter[0] += len(sources)
            send, recv = mem.bulk_send, mem.bulk_recv
            self.out = [
                pltpu.make_async_remote_copy(
                    src_ref=source,
                    dst_ref=target,
                    send_sem=send.at[base + place],
                    recv_sem=recv.at[base + place],
                    device_id={axis: partner},
                    device_id_type=pl.DeviceIdType.MESH,
                )
                for place, (source, target) in enumerate(zip(sources, targets))
            ]
            self.come = [
                pltpu.make_async_remote_copy(
                    src_ref=landing,
                    dst_ref=landing,
                    send_sem=send.at[base + place],
                    recv_sem=recv.at[base + place],
                    device_id={axis: partner},
                    device_id_type=pl.DeviceIdType.MESH,
                )
                for place, landing in enumerate(landings)
            ]

        def start(self):
            for copy in self.out:
                copy.start()

        def arrive(self):
            for copy in self.come:
                copy.wait_recv()

        def leave(self):
            for copy in self.out:
                copy.wait_send()

    class LineBatch:
        def __init__(self, source_of, target_of, landing_of):
            base = counter[0]
            counter[0] += plan.z
            send, recv = mem.bulk_send, mem.bulk_recv
            self.out, self.come = [], []
            for step in range(1, plan.z):
                z_to = (z_me + step) % plan.z
                self.out.append(
                    pltpu.make_async_remote_copy(
                        src_ref=source_of(z_to),
                        dst_ref=target_of(z_to),
                        send_sem=send.at[base + step],
                        recv_sem=recv.at[base + z_me],
                        device_id={FSDP: z_to * plan.x + x_me},
                        device_id_type=pl.DeviceIdType.MESH,
                    )
                )
                self.come.append(
                    pltpu.make_async_remote_copy(
                        src_ref=landing_of(z_to),
                        dst_ref=landing_of(z_to),
                        send_sem=send.at[base + step],
                        recv_sem=recv.at[base + z_to],
                        device_id={FSDP: z_to * plan.x + x_me},
                        device_id_type=pl.DeviceIdType.MESH,
                    )
                )

        start, arrive, leave = Batch.start, Batch.arrive, Batch.leave

    def pick(ref, indexes):
        return [ref.at[index] for index in indexes]

    def own_dp(y_index, c_index):
        return y_index * 2 + c_index

    x_partner = z_me * plan.x + x_other
    y_partner = own_dp(y_other, c_me)
    c_partner = own_dp(y_me, c_other)
    dp_far = own_dp(y_other, c_other)

    class Gather:
        def __init__(self, which, start, size):
            ref = weights[which]
            self.which, self.rows = which, (start, size)
            both, low, high = (start, size), (start, size // 2), (start + size // 2, size // 2)

            def at(*index):
                return pick(ref, places(which, *index, False))

            own = at(z_me, x_me, dp_me, both)[0]
            self.line = LineBatch(
                lambda _: own, lambda _: own, lambda z_from: at(z_from, x_me, dp_me, both)[0]
            )
            sent, come = at(None, x_me, dp_me, low), at(None, x_other, dp_me, low)
            x_first = Batch(sent, sent, come, FSDP, x_partner)
            sent, come = at(None, x_me, dp_me, high), at(None, x_me, y_partner, high)
            y_first = Batch(sent, sent, come, DP, y_partner)
            sent, come = at(None, None, dp_me, low), at(None, None, y_partner, low)
            y_second = Batch(sent, sent, come, DP, y_partner)
            sent = at(None, x_me, dp_me, high) + at(None, x_me, y_partner, high)
            come = at(None, x_other, dp_me, high) + at(None, x_other, y_partner, high)
            x_second = Batch(sent, sent, come, FSDP, x_partner)
            sent = at(None, None, dp_me, both) + at(None, None, y_partner, both)
            come = at(None, None, c_partner, both) + at(None, None, dp_far, both)
            core = Batch(sent, sent, come, DP, c_partner)
            self.stages = ((self.line,), (x_first, y_first), (y_second, x_second), (core,))

        def put_own(self):
            index = places(self.which, z_me, x_me, dp_me, self.rows, False)[0]
            shard = ins.shards[self.which][self.rows[0] : self.rows[0] + self.rows[1], :]
            weights[self.which][index] = shard.astype(bf16)

        def start(self, stage):
            for batch in self.stages[stage]:
                batch.start()

        def arrive(self, stage):
            for batch in self.stages[stage]:
                batch.arrive()

        def leave(self):
            for stage in self.stages:
                for batch in stage:
                    batch.leave()

    class Piece:
        def __init__(self, which, ref, room, z_index):
            def at(*index):
                return pick(ref, places(which, z_index, *index))

            def land(*index):
                return [room(index_one) for index_one in places(which, z_index, *index)]

            self.z = z_index
            self.core = Batch(
                at(None, c_partner, None) + at(None, dp_far, None),
                land(None, c_partner, None) + land(None, dp_far, None),
                land(None, dp_me, None) + land(None, y_partner, None),
                DP,
                c_partner,
            )
            self.y_first = Batch(
                at(None, y_partner, 0), land(None, dp_far, 0), land(None, c_partner, 0), DP, y_partner
            )
            self.x_first = Batch(
                at(x_other, dp_me, 1) + at(x_other, y_partner, 1),
                land(x_other, c_partner, 1) + land(x_other, dp_far, 1),
                land(x_me, c_partner, 1) + land(x_me, dp_far, 1),
                FSDP,
                x_partner,
            )
            self.x_second = Batch(
                at(x_other, dp_me, 0), land(x_other, dp_far, 0), land(x_me, dp_far, 0), FSDP, x_partner
            )
            self.y_second = Batch(
                at(x_me, y_partner, 1), land(x_other, dp_far, 1), land(x_other, c_partner, 1), DP, y_partner
            )

    class Reduce:
        def __init__(self, which, ref, cut):
            self.which, self.ref, self.room = which, ref, recv_parts[which]
            self.pieces = [
                Piece(which, ref, self.room, z_index) for z_index in (range(plan.z) if cut else [None])
            ]
            self.base = counter[0]
            counter[0] += plan.z

        def line_copy(self, z_to):
            return pltpu.make_async_remote_copy(
                src_ref=self.ref.at[places(self.which, z_to, x_me, dp_me, None)[0]],
                dst_ref=self.room(places(self.which, z_me, x_other, dp_far, None)[0]),
                send_sem=mem.bulk_send.at[self.base + z_to],
                recv_sem=mem.bulk_recv.at[self.base + z_me],
                device_id={FSDP: z_to * plan.x + x_me},
                device_id_type=pl.DeviceIdType.MESH,
            )

        def line_room(self, z_from):
            return self.room(places(self.which, z_from, x_other, dp_far, None)[0])

        def add(self, z_index, pairs):
            def one(z_one):
                for here, there in pairs:
                    for x_step in range(plan.x) if here[0] is None else [None]:
                        x_here = x_step if here[0] is None else here[0]
                        x_there = x_step if there[0] is None else there[0]
                        index = places(self.which, z_one, x_here, *here[1:])[0]
                        other = places(self.which, z_one, x_there, *there[1:])[0]
                        total = self.ref[index].astype(f32) + self.room(other)[...].astype(f32)
                        self.ref[index] = total.astype(bf16)

            if z_index is None:
                pl.loop(0, plan.z)(one)
            else:
                one(z_index)

        def core_start(self, place=0):
            if plan.inside:
                self.pieces[place].core.start()

        def core_add(self, place=0):
            if plan.inside:
                piece = self.pieces[place]
                piece.core.arrive()
                self.add(piece.z, [((None, dp_me, None),) * 2, ((None, y_partner, None),) * 2])
                piece.y_first.start()
                piece.x_first.start()

        def first_add(self, place=0):
            if plan.inside:
                piece = self.pieces[place]
                piece.y_first.arrive()
                self.add(piece.z, [((None, dp_me, 0), (None, c_partner, 0))])
                piece.x_second.start()
                piece.x_first.arrive()
                self.add(
                    piece.z, [((x_me, dp_me, 1), (x_me, c_partner, 1)), ((x_me, y_partner, 1), (x_me, dp_far, 1))]
                )
                piece.y_second.start()

        def second_add(self, place=0):
            if plan.inside:
                piece = self.pieces[place]
                piece.x_second.arrive()
                piece.y_second.arrive()
                self.add(
                    piece.z, [((x_me, dp_me, 0), (x_me, dp_far, 0)), ((x_me, dp_me, 1), (x_other, c_partner, 1))]
                )
                if piece.z is None:
                    for step in range(1, plan.z):
                        self.line_copy((z_me + step) % plan.z).start()
                else:

                    @pl.when(z_me != piece.z)
                    def _():
                        self.line_copy(piece.z).start()

        def finish(self):
            if not plan.inside:
                return
            total = self.ref[places(self.which, z_me, x_me, dp_me, None)[0]].astype(f32)
            for step in range(1, plan.z):
                z_from = (z_me + step) % plan.z
                room = self.line_room(z_from)
                pltpu.make_async_remote_copy(
                    src_ref=room,
                    dst_ref=room,
                    send_sem=mem.bulk_send.at[self.base + z_from],
                    recv_sem=mem.bulk_recv.at[self.base + z_from],
                    device_id={FSDP: z_from * plan.x + x_me},
                    device_id_type=pl.DeviceIdType.MESH,
                ).wait_recv()
                total = total + room[...].astype(f32)
            outs.grads[self.which][...] = total
            squares = jnp.sum(total * total, axis=0, keepdims=True)
            folded = squares[:, :LANES]
            for place in range(1, squares.shape[1] // LANES):
                folded = folded + squares[:, place * LANES : (place + 1) * LANES]
            mem.squares[...] += folded
            for step in range(1, plan.z):
                self.line_copy((z_me + step) % plan.z).wait_send()
            for piece in self.pieces:
                for batch in (piece.core, piece.y_first, piece.x_first, piece.x_second, piece.y_second):
                    batch.leave()

    gathers, steps = [], []
    if plan.inside:
        for which, cuts in enumerate((2, 3, 1, 2, 1)):
            size = 2 * plan.half[which] // cuts
            gathers += [Gather(which, cut * size, size) for cut in range(cuts)]

    def line_step(place):
        gathers[place].arrive(0)
        gathers[place].start(1)
        if place + 1 < len(gathers):
            gathers[place + 1].start(0)

    def first_step(place):
        gathers[place].arrive(1)
        gathers[place].start(2)

    def second_step(place):
        gathers[place].arrive(2)
        gathers[place].start(3)

    for place in range(len(gathers)):
        steps.append((line_step, place))
        if place > 0:
            steps.append((second_step, place - 1))
        steps.append((first_step, place))
    if plan.inside:
        steps.append((second_step, len(gathers) - 1))

    def take(count):
        taken, steps[:] = steps[:count], steps[count:]
        return [lambda one=one: one[0](one[1]) for one in taken]

    def advance(count):
        for move in take(count):
            move()

    def cores_arrive(which):
        for one in gathers:
            if one.which == which:
                one.arrive(3)

    gradients = [mem.g1, mem.stage.at[pl.ds(0, 9 * C_MID)], weights[2], weights[3], weights[4]]
    reduces = [Reduce(which, gradients[which], which < 4) for which in range(5)]
    mem.squares[...] = jnp.zeros((1, LANES), f32)

    if plan.inside:
        gathers[0].put_own()
        gathers[0].start(0)
        for one in gathers[1:]:
            one.put_own()
        tiles = mem.norm_tiles
        tiles[dp_me, fsdp_me] = ins.norm[...].astype(bf16).astype(f32)
        norm_dp = share(
            DP, plan.dp, dp_me, lambda _: tiles.at[dp_me, fsdp_me], tiles.at[:, fsdp_me], mem.norm_s0, mem.norm_r0
        )
        norm_dp[0]()
    else:
        loads = [
            pltpu.make_async_copy(ins.shards[which], weights[which], mem.bulk_send.at[which])
            for which in range(5)
        ]
        for load in loads:
            load.start()

    stage_ref, stage_sem = mem.stage, mem.stage_sem
    pieces = BLOCKS * CHUNKS

    def stage_rows(index, pixel=0, count=chunk):
        return pl.ds(pl.multiple_of(lax.rem(index, SLOTS) * chunk + pixel * views, 16), count)

    def hidden_rows(index, pixel=0, count=chunk):
        return pl.ds(pl.multiple_of(index * chunk + pixel * views, 16), count)

    def piece_copy(array, index, into):
        block, place = index // CHUNKS, lax.rem(index, CHUNKS)
        outer = array.at[
            pl.ds(pl.multiple_of(place * chunk, 16), chunk), pl.ds(pl.multiple_of(block * C_MID, LANES), C_MID)
        ]
        inner = stage_ref.at[stage_rows(index)]
        source, target = (outer, inner) if into else (inner, outer)
        return pltpu.make_async_copy(source, target, stage_sem.at[0 if into else 1, lax.rem(index, SLOTS)])

    def first_loads(array):
        for index in range(3):
            piece_copy(array, index, True).start()

    def next_load(array, index):
        @pl.when(index + 3 < pieces)
        def _():
            piece_copy(array, index + 3, True).start()

    def save(array, index):
        piece_copy(array, index, False).start()

        @pl.when(index >= 2)
        def _():
            piece_copy(array, index - 2, False).wait()

    def last_saves(array):
        for index in (pieces - 2, pieces - 1):
            piece_copy(array, index, False).wait()

    def piece_columns(index, part):
        return pl.ds(pl.multiple_of(index // CHUNKS * C_MID + part * LANES, LANES), LANES)

    features, slope_hbm = ins.features, outs.slope
    hidden_three = mem.h3

    def feature_copy(block, target):
        return pltpu.make_async_copy(
            features.at[:, pl.ds(block * C_MID, C_MID)], target, mem.column_sem.at[block]
        )

    feature_loads = [
        feature_copy(block, hidden_three.at[pl.ds(block * rows, rows)]) for block in range(BLOCKS)
    ]
    for copy in feature_loads:
        copy.start()
    first_loads(features)

    padded_one, padded_two = mem.pad1, mem.pad2
    for padded in (padded_one, padded_two):
        for edge in (0, SIDE + 1):
            padded[edge] = jnp.zeros((padded.shape[1], C_MID), bf16)
        for edge in (0, SIDE + 1):
            padded[:, pl.ds(edge * views, views), :] = jnp.zeros((SIDE + 2, views, C_MID), bf16)

    if plan.inside:
        norm_dp[1]()
        norm_out = []
        norm_in = []
        for step in range(1, plan.fsdp):
            partner = (fsdp_me + step) % plan.fsdp
            norm_out.append(
                pltpu.make_async_remote_copy(
                    src_ref=tiles.at[:, fsdp_me],
                    dst_ref=tiles.at[:, fsdp_me],
                    send_sem=mem.norm_s1.at[step],
                    recv_sem=mem.norm_r1.at[fsdp_me],
                    device_id={FSDP: partner},
                    device_id_type=pl.DeviceIdType.MESH,
                )
            )
            norm_in.append(
                pltpu.make_async_remote_copy(
                    src_ref=tiles.at[:, partner],
                    dst_ref=tiles.at[:, partner],
                    send_sem=mem.norm_s1.at[step],
                    recv_sem=mem.norm_r1.at[partner],
                    device_id={FSDP: partner},
                    device_id_type=pl.DeviceIdType.MESH,
                )
            )
        for copy in norm_out:
            copy.start()
        advance(7)
        for copy in norm_in:
            copy.wait_recv()
        for copy in norm_out:
            copy.wait_send()
        norm_all = mem.norm
        for dp_one in range(plan.dp):
            for fsdp_one in range(plan.fsdp):
                start = (dp_one * plan.fsdp + fsdp_one) * LANES
                norm_all[:, start : start + LANES] = tiles[dp_one, fsdp_one]
    else:
        for copy in loads:
            copy.wait()
        norm_all = mem.norm
        norm_all[...] = ins.norm[...]

    starts = (0, C_MID, 2 * C_MID, 2 * C_MID + C_IN, 2 * C_MID + C_IN + P_HID)

    def gain(layer):
        return norm_all[0:1, starts[layer] : starts[layer + 1]]

    coef, stats = mem.coef, mem.stats

    def norm_coefs(layer, totals, count, low=0):
        width = totals.shape[1]
        here, there = slice(low, low + width), slice(starts[layer] + low, starts[layer] + low + width)
        mean = totals[0:1] / count
        scaling = lax.rsqrt(totals[1:2] / count - mean * mean + norm_epsilon)
        slope = scaling * norm_all[0:1, there]
        stats[0:1, there] = mean
        stats[1:2, there] = scaling
        coef[0:1, here] = slope
        coef[1:2, here] = norm_all[1:2, there] - mean * slope

    def grad_coefs(layer, totals, count):
        width = starts[layer + 1] - starts[layer]
        mean = stats[0:1, starts[layer] : starts[layer + 1]]
        scaling = stats[1:2, starts[layer] : starts[layer + 1]]
        outs.norm_grad[0:1, starts[layer] : starts[layer + 1]] = totals[1:2]
        outs.norm_grad[1:2, starts[layer] : starts[layer + 1]] = totals[0:1]
        slope = scaling * gain(layer)
        bend = slope * scaling * totals[1:2] / count
        coef[0:1, :width] = slope
        coef[1:2, :width] = slope * totals[0:1] / count - mean * bend
        coef[2:3, :width] = bend

    def xhat_sum(layer, plain, product):
        mean = stats[0:1, starts[layer] : starts[layer + 1]]
        scaling = stats[1:2, starts[layer] : starts[layer + 1]]
        return scaling * (product - mean * plain)

    zero_row = jnp.zeros((1, C_MID), f32)

    def at_place(index, place, *moves):
        if plan.inside:

            @pl.when(index == place)
            def _():
                for move in moves:
                    move()

    def column_sums(value):
        return jnp.sum(value, axis=0, keepdims=True)

    def whole(which):
        value = weights[which][...]
        return value.reshape(-1, value.shape[-1])

    row_sums = mem.row_sums

    def clear_sums():
        row_sums[...] = jnp.zeros_like(row_sums)

    def count_in(cols, value, other):
        row_sums[0:1, cols] += column_sums(value)
        row_sums[1:2, cols] += column_sums(value * other)

    def own_columns(side):
        core = (c_me + side) % 2
        return [
            pl.ds(pl.multiple_of(half * (C_MID // 2) + core * LANES, LANES), LANES) for half in range(2)
        ]

    hidden_one, slope_one = mem.h1, mem.d1
    hidden_two, slope_two = mem.h2, mem.d2
    act_two = mem.a2
    long = rows // 3

    def span(index):
        return pl.ds(pl.multiple_of(index * chunk, 16), chunk)

    def long_rows(block, index):
        return pl.ds(pl.multiple_of(block * rows + index * long, 16), long)

    def put_sides(ref, at, sides, hidden):
        for place, cols in enumerate(sides):
            part = hidden[:, place * LANES : (place + 1) * LANES]
            ref[at, cols] = part.astype(bf16)
            count_in(cols, part, part)

    for copy in feature_loads:
        copy.wait()
    clear_sums()

    @pl.loop(0, 2)
    def _(side):
        sides = own_columns(side)

        @pl.loop(0, 3)
        def _(index):
            left = jnp.concatenate([hidden_three[long_rows(block, index), :] for block in range(BLOCKS)], axis=1)
            right = jnp.concatenate([weights[0][:, :, :, cols].reshape(C_IN, LANES) for cols in sides], axis=1)
            put_sides(hidden_one, long_rows(0, index), sides, dot(left, right))

            at_place(side * 3 + index, 1, *take(1))
            at_place(side * 3 + index, 3, *take(1))

        at_place(side, 0, lambda: cores_arrive(0))

    sum_one = Sum(0)
    sum_one.start(row_sums[0:1, :C_MID], row_sums[1:2, :C_MID])
    advance(1)
    sum_one.middle()
    advance(1)
    clear_sums()
    norm_coefs(0, sum_one.finish(), row_total)

    def activate(hidden_ref, slope_ref, put):
        @pl.loop(0, PIX)
        def _(pixel):
            place = pl.ds(pl.multiple_of(pixel * views, 16), views)
            for block in range(C_MID // LANES):
                cols = slice(block * LANES, (block + 1) * LANES)
                out = hidden_ref[place, cols].astype(f32) * coef[0:1, cols] + coef[1:2, cols]
                value, slope = gelu_pair(out)
                slope_ref[place, cols] = slope.astype(bf16)
                put(pixel, cols, value.astype(bf16))

    def put_padded(padded):
        def put(pixel, cols, value):
            padded[pixel // SIDE + 1, pl.ds(pl.multiple_of((pixel % SIDE + 1) * views, 16), views), cols] = value

        return put

    activate(hidden_one, slope_one, put_padded(padded_one))
    advance(5)

    def patch(padded, first, count, flip):
        found = []
        for vertical in range(3):
            for lateral in range(3):
                down, across = (2 - vertical, 2 - lateral) if flip else (vertical, lateral)
                piece = padded[pl.ds(first + down, count), across * views : across * views + chunk, :]
                found.append(piece.reshape(count * chunk, C_MID))
        return jnp.concatenate(found, axis=1)

    def image_rows(first, count):
        return pl.ds(pl.multiple_of(first * chunk, 16), count * chunk)

    def second_part(sides, first, count):
        right = jnp.concatenate([weights[1][:, :, :, cols].reshape(9 * C_MID, LANES) for cols in sides], axis=1)
        hidden = dot(patch(padded_one, first, count, False), right)
        put_sides(hidden_two, image_rows(first, count), sides, hidden)

    @pl.loop(0, 2)
    def _(side):
        sides = own_columns(side)

        @pl.loop(0, 3)
        def _(index):
            second_part(sides, 2 * index, 2)
            for place in range(6):
                at_place(side * 3 + index, place, *take(1))

        second_part(sides, 6, 1)
        at_place(side, 0, lambda: cores_arrive(1))

    sum_two = Sum(1)
    sum_two.start(row_sums[0:1, :C_MID], row_sums[1:2, :C_MID])
    sum_two.middle()
    advance(1)
    clear_sums()
    norm_coefs(1, sum_two.finish(), row_total)

    def put_rows(pixel, cols, value):
        act_two[pl.ds(pl.multiple_of(pixel * views, 16), views), cols] = value

    activate(hidden_two, slope_two, put_rows)
    advance(1)
    cores_arrive(2)

    def weight_three(block):
        return weights[2][block].reshape(C_MID, C_MID)

    sums_low, sums_high = Sum(2), Sum(3)
    half_width = C_IN // 2

    @pl.loop(0, BLOCKS)
    def _(block):
        cols = pl.ds(pl.multiple_of(block * C_MID, LANES), C_MID)

        @pl.loop(0, 3)
        def _(index):
            hidden = dot(act_two[long_rows(0, index), :], weight_three(block))
            hidden_three[long_rows(block, index), :] = hidden.astype(bf16)
            count_in(cols, hidden, hidden)

        for place in range(3):
            at_place(block, place, *take(1))

        @pl.when(block == 1)
        def _():
            sums_low.start(row_sums[0:1, :half_width], row_sums[1:2, :half_width])

        @pl.when(block == 2)
        def _():
            sums_low.middle()

    sums_high.start(row_sums[0:1, half_width:], row_sums[1:2, half_width:])
    norm_coefs(2, sums_low.finish(), row_total)

    pool, pool_slope, pool_bend = mem.pool, mem.pool_slope, mem.pool_bend
    for ref in (pool, pool_slope, pool_bend):
        ref[...] = jnp.zeros_like(ref)

    @pl.loop(0, pieces)
    def _(index):
        piece_copy(features, index, True).wait()

        @pl.loop(0, C_MID // LANES)
        def _(part):
            inner = pl.ds(pl.multiple_of(part * LANES, LANES), LANES)
            cols = piece_columns(index, part)
            slope_row, shift_row = coef[0:1, cols], coef[1:2, cols]
            kept = (pool[:, cols], pool_slope[:, cols], pool_bend[:, cols])
            for pixel in range(SIDE):
                stage_at, hidden_at = stage_rows(index, pixel, views), hidden_rows(index, pixel, views)
                hidden = hidden_three[hidden_at, inner].astype(f32)
                total = hidden * slope_row + shift_row + stage_ref[stage_at, inner].astype(f32)
                value, slope = gelu_pair(total)
                stage_ref[stage_at, inner] = slope.astype(bf16)
                kept = (kept[0] + value, kept[1] + slope, kept[2] + slope * hidden)
            pool[:, cols], pool_slope[:, cols], pool_bend[:, cols] = kept

        save(slope_hbm, index)
        next_load(features, index)

        @pl.when(index == 2)
        def _():
            sums_high.middle()

        @pl.when(index == pieces // 2 - 1)
        def _():
            norm_coefs(2, sums_high.finish(), row_total, half_width)

    last_saves(slope_hbm)
    cores_arrive(3)
    cores_arrive(4)
    for one in gathers:
        one.leave()

    pooled = (pool[...] * (1.0 / PIX)).astype(bf16)
    mem.pooled[...] = pooled
    proj_hidden = dot(pooled, whole(3))
    sum_four = Sum(4)
    totals = sum_four.all(column_sums(proj_hidden), column_sums(proj_hidden * proj_hidden))
    first_loads(slope_hbm)
    norm_coefs(3, totals, view_total)
    value, slope = gelu_pair(proj_hidden * coef[0:1, :P_HID] + coef[1:2, :P_HID])
    proj_act = value.astype(bf16)
    mem.proj_act[...] = proj_act
    mem.proj_slope[...] = slope
    mem.proj_hidden[...] = proj_hidden

    def weight_five(block):
        return weights[4][block // plan.x, block % plan.x]

    parts = P_HID // P_OUT
    embedding = jnp.zeros((views, P_OUT), f32)
    for block in range(parts):
        embedding = embedding + dot_cols(proj_act[:, block * P_OUT : (block + 1) * P_OUT], weight_five(block))

    images = views // 2
    order = jnp.broadcast_to(ins.order[...], (images, views))
    image_row = lax.broadcasted_iota(jnp.int32, (images, views), 0)
    selectors = [(order == 2 * image_row + which).astype(f32) for which in range(2)]
    embeds = [exact_dot(selector, embedding) for selector in selectors]
    moments = [exact_rows(embed, embed) for embed in embeds]
    packed, diagonal = pack_pair(*moments)
    packed, extra = sum_matrix(0, packed, [diagonal] + [column_sums(embed) for embed in embeds])
    moments = unpack_pair(packed, extra[0])
    eye = (
        lax.broadcasted_iota(jnp.int32, (P_OUT, P_OUT), 0) == lax.broadcasted_iota(jnp.int32, (P_OUT, P_OUT), 1)
    ).astype(f32)
    centred, covariances = [], []
    for which in range(2):
        mean = extra[1 + which] / image_total
        centred.append(embeds[which] - mean)
        covariances.append(moments[which] / image_total - exact_rows(mean, mean) + ridge_term * eye)
    inverses = inverse_factors(covariances)
    whitened = [exact_cols(centred[which], inverses[which]) for which in range(2)]
    scalings = [
        lax.rsqrt(jnp.mean(white * white, axis=1, keepdims=True) + norm_epsilon) for white in whitened
    ]
    units = [white * scaling for white, scaling in zip(whitened, scalings)]
    difference = units[0] - units[1]
    objective_row = column_sums(difference * difference) * (1.0 / P_OUT)
    unit_grads = [difference * (2.0 / P_OUT), difference * (-2.0 / P_OUT)]
    white_grads = []
    for which in range(2):
        inner = jnp.mean(whitened[which] * unit_grads[which], axis=1, keepdims=True)
        white_grads.append(
            scalings[which] * unit_grads[which] - whitened[which] * (scalings[which] ** 3 * inner)
        )
    directs = [exact_dot(white_grads[which], inverses[which]) for which in range(2)]
    products = [exact_rows(white_grads[which], whitened[which]) for which in range(2)]
    packed, diagonal = pack_pair(*products)
    packed, extra = sum_matrix(
        1, packed, [diagonal] + [column_sums(grad) for grad in white_grads] + [objective_row]
    )
    products = unpack_pair(packed, extra[0])
    embed_grad = jnp.zeros((views, P_OUT), f32)
    for which in range(2):
        symmetric = exact_rows(inverses[which], exact_dot(products[which], inverses[which]))
        mean_grad = exact_dot(extra[1 + which], inverses[which])
        grad = directs[which] - (exact_dot(centred[which], symmetric) + mean_grad) / image_total
        embed_grad = embed_grad + exact_rows(selectors[which], grad)
    objective_row = extra[3]
    embed_low = embed_grad.astype(bf16)

    proj_act, proj_hidden = mem.proj_act[...], mem.proj_hidden[...]
    act_grad = jnp.concatenate([dot(embed_low, weight_five(block)) for block in range(parts)], axis=1)
    upstream = act_grad * mem.proj_slope[...]
    plain = column_sums(upstream)
    sum_four_back = Sum(5)
    sum_four_back.start(plain, xhat_sum(3, plain, column_sums(upstream * proj_hidden)))
    for block in range(parts):
        weights[4][block // plan.x, block % plan.x] = dot_rows(
            embed_low, proj_act[:, block * P_OUT : (block + 1) * P_OUT]
        ).astype(bf16)
    sum_four_back.middle()
    reduces[4].core_start()
    grad_coefs(3, sum_four_back.finish(), view_total)
    four_low = (
        upstream * coef[0:1, :P_HID] - coef[1:2, :P_HID] - proj_hidden * coef[2:3, :P_HID]
    ).astype(bf16)
    pool_grad = dot_cols(four_low, whole(3)) * (1.0 / PIX)
    plain = column_sums(pool_grad * pool_slope[...])
    sum_three_back = Sum(6)
    sum_three_back.start(plain, xhat_sum(2, plain, column_sums(pool_grad * pool_bend[...])))
    grad_four = dot_rows(mem.pooled[...], four_low).astype(bf16)
    weights[3][...] = grad_four.reshape(weights[3].shape)
    sum_three_back.middle()
    four, three, two, one = reduces[3], reduces[2], reduces[1], reduces[0]
    for place in range(plan.z):
        four.core_start(place)
    grad_coefs(2, sum_three_back.finish(), row_total)
    pool[...] = pool_grad * coef[0:1, :]
    pool_slope[...] = pool_grad

    clear_sums()

    @pl.loop(0, pieces)
    def _(index):
        piece_copy(slope_hbm, index, True).wait()
        next_load(slope_hbm, index)

        @pl.loop(0, C_MID // LANES)
        def _(part):
            inner = pl.ds(pl.multiple_of(part * LANES, LANES), LANES)
            cols = piece_columns(index, part)
            spread, shift_row, bend_row = pool[:, cols], coef[1:2, cols], coef[2:3, cols]
            for pixel in range(SIDE):
                hidden_at = hidden_rows(index, pixel, views)
                hidden = hidden_three[hidden_at, inner].astype(f32)
                slope = stage_ref[stage_rows(index, pixel, views), inner].astype(f32)
                hidden_three[hidden_at, inner] = (slope * spread - shift_row - hidden * bend_row).astype(bf16)

        at_place(index, 3, reduces[4].core_add, lambda: four.core_add(0))
        at_place(index, 11, lambda: four.core_add(1), reduces[4].first_add)
        at_place(index, 20, lambda: four.first_add(0), lambda: four.core_add(2))

    @pl.loop(0, 3)
    def _(index):
        at = long_rows(0, index)
        left = jnp.concatenate([hidden_three[long_rows(block, index), :] for block in range(BLOCKS)], axis=1)
        right = jnp.concatenate([weight_three(block) for block in range(BLOCKS)], axis=1)
        upstream = dot_cols(left, right) * slope_two[at, :].astype(f32)
        slope_two[at, :] = upstream.astype(bf16)
        count_in(slice(0, C_MID), upstream, hidden_two[at, :].astype(f32))
        at_place(index, 0, lambda: four.first_add(1), lambda: four.second_add(0), reduces[4].second_add)
        at_place(index, 1, lambda: four.core_add(3))
        at_place(index, 2, lambda: four.first_add(2), lambda: four.second_add(1))

    sums = row_sums[0:1, :C_MID], row_sums[1:2, :C_MID]
    sum_two_back = Sum(7)
    sum_two_back.start(sums[0], xhat_sum(1, *sums))

    @pl.loop(0, BLOCKS)
    def _(block):
        three = hidden_three[pl.ds(pl.multiple_of(block * rows, 16), rows), :]
        grad = dot_rows(act_two[...], three)
        weights[2][block] = grad.astype(bf16).reshape(plan.z, plan.x, -1, C_MID)

        @pl.when(block == 1)
        def _():
            sum_two_back.middle()

        at_place(block, 0, lambda: four.first_add(3))
        at_place(block, 2, lambda: four.second_add(2))
        at_place(block, 3, lambda: four.second_add(3))

    for place in range(plan.z):
        three.core_start(place)
    clear_sums()
    grad_coefs(1, sum_two_back.finish(), row_total)

    def apply_grad(hidden_ref, grad_ref, put):
        @pl.loop(0, PIX)
        def _(pixel):
            place = pl.ds(pl.multiple_of(pixel * views, 16), views)
            for block in range(C_MID // LANES):
                cols = slice(block * LANES, (block + 1) * LANES)
                grad = (
                    grad_ref[place, cols].astype(f32) * coef[0:1, cols]
                    - coef[1:2, cols]
                    - hidden_ref[place, cols].astype(f32) * coef[2:3, cols]
                )
                put(pixel, cols, grad.astype(bf16))

    apply_grad(hidden_two, slope_two, put_padded(padded_two))
    reduces[4].finish()
    column_places = [
        hidden_three.at[pl.ds(2 * rows, rows)],
        hidden_three.at[pl.ds(3 * rows, rows)],
        hidden_two,
        slope_two,
    ]
    column_loads = [feature_copy(block, column_places[block]) for block in range(BLOCKS)]
    for copy in column_loads:
        copy.start()
    three.core_add(0)
    three.core_add(1)

    def tap_grad(tap):
        down, across = tap // 3, tap % 3
        left = padded_one[pl.ds(down, SIDE), pl.ds(pl.multiple_of(across * views, 16), chunk), :]
        right = padded_two[1 : SIDE + 1, views : views + chunk, :]
        grad = dot_rows(left.reshape(rows, C_MID), right.reshape(rows, C_MID))
        stage_ref[pl.ds(pl.multiple_of(tap * C_MID, 16), C_MID), :] = grad.astype(bf16)

    pl.loop(0, 3)(tap_grad)
    two.core_start(0)
    three.first_add(0)
    three.core_add(2)
    three.core_add(3)
    pl.loop(3, 5)(tap_grad)
    two.core_start(1)
    two.core_add(0)
    three.first_add(1)
    three.second_add(0)
    pl.loop(5, 7)(tap_grad)
    two.core_start(2)
    three.first_add(2)
    three.first_add(3)
    two.core_add(1)
    three.second_add(1)
    four.finish()

    def second_back(first, count):
        flat = weights[1][...].reshape(9 * C_MID, C_MID)
        right = jnp.concatenate([flat[tap * C_MID : (tap + 1) * C_MID, :] for tap in range(9)], axis=1)
        at = image_rows(first, count)
        upstream = dot_cols(patch(padded_two, first, count, True), right) * slope_one[at, :].astype(f32)
        slope_one[at, :] = upstream.astype(bf16)
        count_in(slice(0, C_MID), upstream, hidden_one[at, :].astype(f32))

    @pl.loop(0, 3)
    def _(index):
        second_back(2 * index, 2)
        at_place(
            index, 0, lambda: two.first_add(0), lambda: two.core_add(2), lambda: three.second_add(2), lambda: three.second_add(3)
        )
        at_place(index, 1, lambda: two.first_add(1), three.finish, lambda: two.second_add(0))
        at_place(index, 2, lambda: two.first_add(2), lambda: two.second_add(1))

    second_back(6, 1)
    sums = row_sums[0:1, :C_MID], row_sums[1:2, :C_MID]
    sum_one_back = Sum(8)
    sum_one_back.start(sums[0], xhat_sum(0, *sums))

    @pl.loop(7, 9)
    def _(tap):
        tap_grad(tap)

        @pl.when(tap == 7)
        def _():
            sum_one_back.middle()

    two.core_start(3)
    two.second_add(2)
    grad_coefs(0, sum_one_back.finish(), row_total)

    def put_one(pixel, cols, value):
        act_two[pl.ds(pl.multiple_of(pixel * views, 16), views), cols] = value

    apply_grad(hidden_one, slope_one, put_one)
    two.core_add(3)

    def block_grad(block):
        column_loads[block].wait()
        grad = dot_rows(column_places[block][...], act_two[...])
        mem.g1[block] = grad.astype(bf16).reshape(plan.x, -1, C_MID)

    block_grad(0)
    one.core_start(0)
    two.first_add(3)
    block_grad(1)
    one.core_start(1)
    one.core_add(0)
    two.second_add(3)
    block_grad(2)
    one.core_start(2)
    one.core_add(1)
    one.first_add(0)
    block_grad(3)
    one.core_start(3)
    one.core_add(2)
    one.first_add(1)
    one.second_add(0)
    two.finish()

    first_loads(slope_hbm)
    sum_last = Sum(9)

    @pl.loop(0, pieces)
    def _(index):
        block = index // CHUNKS
        weight = weights[0][block].reshape(C_MID, C_MID)
        back = dot_cols(act_two[span(lax.rem(index, CHUNKS)), :], weight)
        piece_copy(slope_hbm, index, True).wait()
        cols = pl.ds(pl.multiple_of(block * C_MID, LANES), C_MID)
        for pixel in range(SIDE):
            at = stage_rows(index, pixel, views)
            summed = stage_ref[at, :].astype(f32) * pool_slope[:, cols]
            stage_ref[at, :] = (summed + back[pixel * views : (pixel + 1) * views]).astype(bf16)
        save(outs.features_grad, index)
        next_load(slope_hbm, index)
        at_place(index, 2, lambda: one.core_add(3), lambda: one.first_add(2), lambda: one.second_add(1))
        at_place(index, 8, lambda: one.first_add(3), lambda: one.second_add(2))
        at_place(index, 13, lambda: one.second_add(3))
        at_place(index, 20, one.finish, lambda: sum_last.start(mem.squares[...], mem.squares[...]))
        at_place(index, 24, sum_last.middle)

    last_saves(outs.features_grad)
    squares = mem.squares[...]
    if plan.inside:
        squares = sum_last.finish()[0:1]
    norm_grads = outs.norm_grad[...]
    scalars = outs.scalars
    norm_squares = column_sums(norm_grads * norm_grads)
    for place in range(norm_squares.shape[1] // LANES):
        squares = squares + norm_squares[:, place * LANES : (place + 1) * LANES]
    scalars[...] = jnp.zeros_like(scalars)
    scalars[0:1, :] = jnp.broadcast_to(jnp.sum(objective_row, axis=1, keepdims=True) / image_total, (1, LANES))
    scalars[1:2, :] = jnp.broadcast_to(jnp.sum(squares, axis=1, keepdims=True), (1, LANES))
    if not plan.inside:
        stores = [
            pltpu.make_async_copy(gradients[which], outs.grads[which], mem.bulk_send.at[which])
            for which in range(5)
        ]
        for store in stores:
            store.start()
        for store in stores:
            store.wait()


def weight_shapes():
    return (
        (4, 2, 256, C_MID),
        (4, 2, 576, C_MID),
        (BLOCKS, 4, 2, 64, C_MID),
        (4, 2, 256, P_HID),
        (4, 2, P_OUT, P_OUT),
    )


def run_kernel(plan, features, order, shards, norm):
    rows, views = plan.rows, plan.views
    in_vmem = pl.BlockSpec(memory_space=pltpu.VMEM)
    anywhere = pl.BlockSpec(memory_space=pl.ANY)
    shapes = weight_shapes()
    operands = [features, order, norm, *shards]
    in_specs = [anywhere, in_vmem, in_vmem] + [in_vmem if plan.inside else anywhere] * 5
    results = [
        ((rows, C_IN), bf16, anywhere),
        ((rows, C_IN), bf16, anywhere),
        ((2, norm_width()), f32, in_vmem),
        ((8, LANES), f32, in_vmem),
    ]
    for which, shard in enumerate(shards):
        if plan.inside:
            results.append((shard.shape, f32, in_vmem))
        else:
            results.append(((9 * C_MID, C_MID) if which == 1 else shapes[which], bf16, anywhere))
    dma = pltpu.SemaphoreType.DMA

    def sum_room(width):
        return SumRoom(
            pltpu.VMEM((plan.dp, 2, width), f32),
            pltpu.VMEM((plan.fsdp, 2, width), f32),
            dma((plan.dp,)),
            dma((plan.dp,)),
            dma((plan.fsdp,)),
            dma((plan.fsdp,)),
        )

    def matrix_room():
        size = plan.embed_rows
        return MatrixRoom(
            pltpu.VMEM((plan.dp, size, P_OUT), f32),
            pltpu.VMEM((plan.dp, size, P_OUT), f32),
            pltpu.VMEM((plan.fsdp, size, P_OUT), f32),
            pltpu.VMEM((plan.dp, size, P_OUT), f32),
            dma((plan.dp,)),
            dma((plan.dp,)),
            dma((plan.fsdp,)),
            dma((plan.fsdp,)),
            dma((plan.dp,)),
            dma((plan.dp,)),
        )

    scratch = Mem(
        w=[pltpu.VMEM(shape, bf16) for shape in shapes],
        g1=pltpu.VMEM(shapes[0], bf16),
        row_sums=pltpu.VMEM((2, C_IN), f32),
        r3=pltpu.VMEM(shapes[2], bf16),
        r4=pltpu.VMEM(shapes[3], bf16),
        r5=pltpu.VMEM(shapes[4], bf16),
        stage=pltpu.VMEM((max(SLOTS * plan.chunk, 9 * C_MID), C_MID), bf16),
        stage_sem=dma((2, SLOTS)),
        column_sem=dma((BLOCKS,)),
        h1=pltpu.VMEM((rows, C_MID), bf16),
        d1=pltpu.VMEM((rows, C_MID), bf16),
        h2=pltpu.VMEM((rows, C_MID), bf16),
        d2=pltpu.VMEM((rows, C_MID), bf16),
        a2=pltpu.VMEM((rows, C_MID), bf16),
        h3=pltpu.VMEM((BLOCKS * rows, C_MID), bf16),
        pad1=pltpu.VMEM((SIDE + 2, (SIDE + 2) * views, C_MID), bf16),
        pad2=pltpu.VMEM((SIDE + 2, (SIDE + 2) * views, C_MID), bf16),
        pool=pltpu.VMEM((views, C_IN), f32),
        pool_slope=pltpu.VMEM((views, C_IN), f32),
        pool_bend=pltpu.VMEM((views, C_IN), f32),
        pooled=pltpu.VMEM((views, C_IN), bf16),
        proj_act=pltpu.VMEM((views, P_HID), bf16),
        proj_slope=pltpu.VMEM((views, P_HID), f32),
        proj_hidden=pltpu.VMEM((views, P_HID), f32),
        coef=pltpu.VMEM((8, C_IN), f32),
        stats=pltpu.VMEM((2, norm_width()), f32),
        norm=pltpu.VMEM((2, norm_width()), f32),
        norm_tiles=pltpu.VMEM((plan.dp, plan.fsdp, 2, LANES), f32),
        norm_s0=dma((plan.dp,)),
        norm_r0=dma((plan.dp,)),
        norm_s1=dma((plan.fsdp,)),
        norm_r1=dma((plan.fsdp,)),
        bulk_send=dma((300,)),
        bulk_recv=dma((300,)),
        mats=[matrix_room(), matrix_room()],
        sums=[
            sum_room(width)
            for width in (C_MID, C_MID, C_IN // 2, C_IN // 2, P_HID, C_IN, LANES)
        ],
        squares=pltpu.VMEM((1, LANES), f32),
    )
    values = pl.pallas_call(
        lambda *refs: kernel(plan, *refs),
        out_shape=[jax.ShapeDtypeStruct(shape, kind) for shape, kind, _ in results],
        in_specs=in_specs,
        out_specs=[spec for _, _, spec in results],
        scratch_shapes=[scratch],
        compiler_params=pltpu.CompilerParams(
            collective_id=1, has_side_effects=True, vmem_limit_bytes=63 * 2**20
        ),
        name="train_step",
    )(*operands)
    return Outs(*values[:4], values[4:])


def norm_width():
    return 2 * C_MID + C_IN + P_HID


def adam_update(weight, moment_one, moment_two, gradient, step_rate, weight_decay):
    first_new = beta_first * moment_one + (1.0 - beta_first) * gradient
    second_new = beta_second * moment_two + (1.0 - beta_second) * gradient * gradient
    first_hat = first_new / (1.0 - beta_first**STEP)
    second_hat = second_new / (1.0 - beta_second**STEP)
    weight_new = weight - step_rate * (
        first_hat / (jnp.sqrt(second_hat) + adam_epsilon) + weight_decay * weight
    )
    return (weight_new, first_new, second_new)


def finish_kernel(rates, decays, *refs):
    count = len(rates)
    low, factor = refs[0], refs[1]
    given, results = refs[2 : 2 + 4 * count], refs[2 + 4 * count :]
    results[0][...] = low[...].astype(f32)

    @pl.when(pl.program_id(0) == 0)
    def _():
        scale = factor[0, 0]
        for place in range(count):
            weight, first, second, grad = (given[part * count + place][...] for part in range(4))
            updated = adam_update(weight, first, second, grad * scale, rates[place], decays[place])
            for part in range(3):
                results[1 + part * count + place][...] = updated[part]


def finish(features_grad, factor, masters, firsts, seconds, grads, rates, decays):
    rows = features_grad.shape[0]
    arrays = [*masters, *firsts, *seconds, *grads]

    def fixed(shape):
        return pl.BlockSpec(shape, lambda index: (0, 0))

    step = rows // CHUNKS
    moving = pl.BlockSpec((step, C_IN), lambda index: (index, 0))
    outputs = [*masters] * 3
    values = pl.pallas_call(
        lambda *refs: finish_kernel(rates, decays, *refs),
        grid=(CHUNKS,),
        in_specs=[moving, pl.BlockSpec(memory_space=pltpu.SMEM)] + [fixed(array.shape) for array in arrays],
        out_specs=[moving] + [fixed(array.shape) for array in outputs],
        out_shape=[jax.ShapeDtypeStruct((rows, C_IN), f32)]
        + [jax.ShapeDtypeStruct(array.shape, f32) for array in outputs],
        compiler_params=pltpu.CompilerParams(vmem_limit_bytes=62 * 2**20),
        name="finish",
    )(features_grad, factor, *arrays)
    count = len(masters)
    return values[0], values[1 : 1 + count], values[1 + count : 1 + 2 * count], values[1 + 2 * count :]


def gather_full(weight):
    outer = lax.all_gather(weight.astype(bf16), FSDP, axis=0, tiled=True)
    return lax.all_gather(outer, DP, axis=1, tiled=True)


def scatter_full(gradient):
    inner = lax.psum_scatter(gradient.astype(f32), DP, scatter_dimension=1, tiled=True)
    return lax.psum_scatter(inner, FSDP, scatter_dimension=0, tiled=True)


def body(features, view_order, *state):
    masters, firsts, seconds = state[:6], state[6:12], state[12:18]
    dp_size, fsdp_size = lax.axis_size(DP), lax.axis_size(FSDP)
    views = features.shape[0]
    inside = dp_size == 4 and fsdp_size == 8
    plan = Plan(dp_size, fsdp_size, views, inside)
    pixels = jnp.swapaxes(features, 0, 1).reshape(-1, C_IN)
    norm_params = masters[5]
    shapes = weight_shapes()
    if inside:
        shards = list(masters[:4]) + [masters[4].T]
        norm = norm_params
    else:
        full = [gather_full(weight) for weight in masters[:5]]
        shards = [
            full[0].reshape(shapes[0]),
            full[1].reshape(shapes[1]),
            full[2].reshape(C_MID, BLOCKS, C_MID).swapaxes(0, 1).reshape(shapes[2]),
            full[3].reshape(shapes[3]),
            full[4].reshape(4, 2, P_OUT, P_OUT).swapaxes(2, 3),
        ]
        norm = lax.all_gather(norm_params.astype(bf16), (DP, FSDP), axis=1, tiled=True).astype(f32)
    got = run_kernel(plan, pixels, view_order, shards, norm)
    grads = list(got.grads)
    squares = got.scalars[1, 0]
    turned = [list(group) for group in (masters, firsts, seconds)]
    if inside:
        owned = grads
        for group in turned:
            group[4] = group[4].T
    else:
        whole_grads = [
            grads[0].reshape(C_IN, C_MID),
            grads[1],
            grads[2].reshape(BLOCKS, C_MID, C_MID).swapaxes(0, 1).reshape(C_MID, C_IN),
            grads[3].reshape(C_IN, P_HID),
            grads[4].swapaxes(2, 3).reshape(P_HID, P_OUT),
        ]
        owned = [scatter_full(gradient) for gradient in whole_grads]
        squares = squares + lax.psum(sum(jnp.sum(grad * grad) for grad in owned), (DP, FSDP))
    width = norm_params.shape[1]
    owner = lax.axis_index((DP, FSDP))
    owned.append(lax.dynamic_slice_in_dim(got.norm_grad, owner * width, width, 1))
    grad_norm = jnp.sqrt(squares)
    factor = clip_level / jnp.maximum(grad_norm, clip_level)
    step_rates = (
        C_IN ** (-0.5),
        (9 * C_MID) ** (-0.5),
        C_MID ** (-0.5),
        C_IN ** (-0.5),
        P_HID ** (-0.5),
        norm_rate,
    )
    decays = (decay_rate, decay_rate, decay_rate, decay_rate, decay_rate, 0.0)
    input_grad, *updates = finish(
        got.features_grad, factor.reshape(1, 1), *turned, owned, step_rates, decays
    )
    if inside:
        updates = [[*group[:4], group[4].T, group[5]] for group in updates]
    return (
        got.scalars[0, 0],
        jnp.swapaxes(input_grad.reshape(PIX, views, C_IN), 0, 1),
        grad_norm,
        *updates[0],
        *updates[1],
        *updates[2],
    )


def solution(mesh):
    views = P((DP, FSDP), None, None)
    split = P(FSDP, DP)
    norm = P(None, (DP, FSDP))
    params = (split,) * 5 + (norm,)
    return jax.shard_map(
        body,
        mesh=mesh,
        in_specs=(views, P((DP, FSDP), None)) + params * 3,
        out_specs=(P(), views, P()) + params * 3,
        check_vma=False,
    )
```

profile of v0, /device:TPU:0, one launch (start us, length us, event | category | flops | bytes accessed | tf_op | source)
XLA Modules:
  0.0 304.6 jit_solution(3087480001942075513)
XLA Ops:
  0.7 285.8 %train_step.1 = (bf16[2352,2048]{1,0:T(8,128)(2,1)}, bf16[2352,2048]{1,0:T(8,128)(2,1)}, f32[2,4096]{1,0:T(2,128)}, f32[8,128]{1,0:T(8,128)}, f32[256,128]{1,0:T...) custom-call(bf16[2352,2048]{1,0:T(8,128)(2,1)} %bitcast.15, ...), custom_call_target="tpu_custom_call" | custom-call | tf_op jit(solution)/shard_map/train_step/pallas_call | solution.py:1487
  286.4 1.3 fusion
  288.4 1.2 constant_dynamic-slice_fusion.refs_25_
  289.7 13.8 %finish.1 = (f32[2352,2048]{1,0:T(8,128)}, f32[256,128]{1,0:T(8,128)}, f32[576,128]{1,0:T(8,128)}, f32[64,512]{1,0:T(8,128)}, f32[256,256]{1,0:T(8,128)}, /*inde...) custom-call(bf16[2352,2048]{1,0:T(8,128)(2,1)} %get-tuple-element.49, ...), custom_call_target="tpu_custom_call" | custom-call | tf_op jit(solution)/shard_map/finish/pallas_call | solution.py:1542
where the time goes:
time: 305 us
  Pallas kernels  300 us (98%)
    pallas_call x1, Pallas kernels, run_kernel(): pl.pallas_call(lambda *refs: kernel(plan, *refs), out_shape=[jax.ShapeDty...  286 us
    pallas_call x1, Pallas kernels, finish(): pl.pallas_call(lambda *refs: finish_kernel(rates, decays, *refs), grid=(C...  13.8 us

commit v1 on v0

--- a/solution.py
+++ b/solution.py
@@ -18,6 +18,7 @@
 BLOCKS = C_IN // C_MID
 CHUNKS = SIDE
 SLOTS = 6
+LAST_SUM = 23
 
 
 highest = lax.Precision.HIGHEST
@@ -103,9 +104,15 @@
             for left, right in pairs
         )
 
-    start = tuple((matrix, (row_all == col_all).astype(f32)) for matrix in matrices)
-    done = lax.fori_loop(0, P_OUT // 8, panel, start)
-    return [right for _, right in done]
+    pairs = tuple((matrix, (row_all == col_all).astype(f32)) for matrix in matrices)
+    done = [[] for _ in matrices]
+    size = P_OUT // 4
+    for _ in range(4):
+        pairs = lax.fori_loop(0, size // 8, panel, pairs)
+        for found, (_, right) in zip(done, pairs):
+            found.append(right[-size:])
+        pairs = tuple((left[:-size], right[:-size]) for left, right in pairs)
+    return [jnp.concatenate(found, axis=0) for found in done]
 
 
 def pack_pair(first, second):
@@ -123,6 +130,76 @@
     first = jnp.where(row >= col, packed, turned)
     second = jnp.where(row < col, packed, jnp.where(row == col, diagonal, turned))
     return first, second
+
+
+GATHER_AT = {
+    (0, 1): 1,
+    (0, 3): 1,
+    (1, 0): 1,
+    (3, 0): 1,
+    (3, 2): 1,
+    (3, 3): 1,
+    (3, 6): 1,
+    (5, 1): 1,
+    (5, 4): 1,
+    (6, 0): 2,
+    (9, 4): 1,
+    (9, 11): 1,
+    (10, 0): 1,
+    (10, 7): 1,
+    (10, 15): 2,
+    (10, 21): 1,
+    (21, 0): 9,
+}
+REDUCE_AT = {
+    (11, 0): ((4, 0, 0),),
+    (11, 6): ((3, 2, 0),),
+    (11, 7): ((3, 3, 0),),
+    (11, 13): ((3, 0, 0),),
+    (11, 17): ((3, 1, 1),),
+    (11, 21): ((4, 0, 1),),
+    (11, 25): ((3, 2, 1),),
+    (12, 2): ((3, 3, 1), (3, 1, 2)),
+    (13, 2): ((3, 0, 1),),
+    (13, 3): ((2, 0, 0),),
+    (14, 1): ((3, 2, 2),),
+    (14, 2): ((3, 3, 2),),
+    (14, 4): ((3, 1, 3), (2, 2, 0)),
+    (14, 6): ((2, 3, 0), (2, 1, 0)),
+    (15, 0): ((2, 0, 1),),
+    (15, 1): ((3, 0, 2),),
+    (15, 2): ((4, 0, 2),),
+    (15, 3): ((2, 3, 1),),
+    (15, 4): ((1, 1, 0),),
+    (15, 5): ((1, 0, 0), (2, 2, 1), (2, 1, 1)),
+    (15, 6): ((3, 3, 3), (3, 2, 3)),
+    (16, 0): ((2, 0, 2), (2, 2, 2), (1, 1, 1), (1, 2, 0)),
+    (16, 1): ((3, 0, 3), (2, 1, 2), (1, 0, 1)),
+    (16, 2): ((2, 3, 2),),
+    (16, 3): ((3, 9, 4), (2, 0, 3), (1, 2, 1)),
+    (17, 0): ((2, 1, 3),),
+    (17, 1): ((1, 3, 0), (1, 0, 2), (2, 3, 3), (2, 2, 3)),
+    (18, 0): ((1, 1, 2),),
+    (18, 4): ((4, 0, 3),),
+    (18, 5): ((1, 3, 1),),
+    (19, 0): ((2, 9, 4), (1, 0, 3), (1, 1, 3), (1, 2, 2)),
+    (19, 1): ((0, 1, 0), (0, 0, 0), (1, 3, 2)),
+    (19, 2): ((1, 2, 3), (0, 1, 1), (0, 2, 0)),
+    (19, 3): ((0, 0, 1),),
+    (20, 0): ((0, 3, 0),),
+    (20, 2): ((0, 2, 1),),
+    (20, 4): ((0, 1, 2), (1, 3, 3)),
+    (20, 6): ((0, 3, 1),),
+    (20, 8): ((0, 2, 2),),
+    (20, 10): ((0, 0, 2), (0, 1, 3)),
+    (20, 12): ((4, 9, 4),),
+    (20, 13): ((0, 3, 2),),
+    (20, 14): ((0, 2, 3),),
+    (20, 17): ((0, 0, 3), (1, 9, 4)),
+    (20, 18): ((0, 3, 3),),
+    (20, 22): ((0, 9, 4),),
+    (23, 0): ((3, 1, 0),),
+}
 
 
 class Ins(NamedTuple):
@@ -190,6 +267,7 @@
     coef: Any
     stats: Any
     norm: Any
+    norm_grads: Any
     norm_tiles: Any
     norm_s0: Any
     norm_r0: Any
@@ -687,9 +765,35 @@
         taken, steps[:] = steps[:count], steps[count:]
         return [lambda one=one: one[0](one[1]) for one in taken]
 
-    def advance(count):
-        for move in take(count):
+    def moves(site, item):
+        found = take(GATHER_AT.get((site, item), 0)) if plan.inside else []
+        for which, piece, kind in REDUCE_AT.get((site, item), ()):
+            one = reduces[which]
+            found.append(
+                one.finish
+                if kind == 4
+                else lambda one=one, kind=kind, piece=piece: (
+                    one.core_start,
+                    one.core_add,
+                    one.first_add,
+                    one.second_add,
+                )[kind](piece)
+            )
+        return found
+
+    def hook(site, item=0):
+        for move in moves(site, item):
             move()
+
+    def hook_in(site, index, count, first=0, stride=1):
+        for item in range(count):
+            found = moves(site, item)
+            if found and plan.inside:
+
+                @pl.when(index == first + item * stride)
+                def _(found=found):
+                    for move in found:
+                        move()
 
     def cores_arrive(which):
         for one in gathers:
@@ -719,43 +823,54 @@
         for load in loads:
             load.start()
 
-    stage_ref, stage_sem = mem.stage, mem.stage_sem
     pieces = BLOCKS * CHUNKS
-
-    def stage_rows(index, pixel=0, count=chunk):
-        return pl.ds(pl.multiple_of(lax.rem(index, SLOTS) * chunk + pixel * views, 16), count)
 
     def hidden_rows(index, pixel=0, count=chunk):
         return pl.ds(pl.multiple_of(index * chunk + pixel * views, 16), count)
 
-    def piece_copy(array, index, into):
-        block, place = index // CHUNKS, lax.rem(index, CHUNKS)
-        outer = array.at[
-            pl.ds(pl.multiple_of(place * chunk, 16), chunk), pl.ds(pl.multiple_of(block * C_MID, LANES), C_MID)
-        ]
-        inner = stage_ref.at[stage_rows(index)]
-        source, target = (outer, inner) if into else (inner, outer)
-        return pltpu.make_async_copy(source, target, stage_sem.at[0 if into else 1, lax.rem(index, SLOTS)])
-
-    def first_loads(array):
-        for index in range(3):
-            piece_copy(array, index, True).start()
-
-    def next_load(array, index):
-        @pl.when(index + 3 < pieces)
-        def _():
-            piece_copy(array, index + 3, True).start()
-
-    def save(array, index):
-        piece_copy(array, index, False).start()
-
-        @pl.when(index >= 2)
-        def _():
-            piece_copy(array, index - 2, False).wait()
-
-    def last_saves(array):
-        for index in (pieces - 2, pieces - 1):
-            piece_copy(array, index, False).wait()
+    class Ring:
+        def __init__(self, ref, start):
+            self.ref, self.base = ref, start
+
+        def rows(self, index, pixel=0, count=chunk):
+            return pl.ds(
+                pl.multiple_of(self.base + lax.rem(index, SLOTS) * chunk + pixel * views, 16), count
+            )
+
+        def copy(self, array, index, into):
+            block, place = index // CHUNKS, lax.rem(index, CHUNKS)
+            outer = array.at[
+                pl.ds(pl.multiple_of(place * chunk, 16), chunk),
+                pl.ds(pl.multiple_of(block * C_MID, LANES), C_MID),
+            ]
+            inner = self.ref.at[self.rows(index)]
+            source, target = (outer, inner) if into else (inner, outer)
+            return pltpu.make_async_copy(
+                source, target, mem.stage_sem.at[0 if into else 1, lax.rem(index, SLOTS)]
+            )
+
+        def first_loads(self, array):
+            for index in range(3):
+                self.copy(array, index, True).start()
+
+        def next_load(self, array, index):
+            @pl.when(index + 3 < pieces)
+            def _():
+                self.copy(array, index + 3, True).start()
+
+        def save(self, array, index):
+            self.copy(array, index, False).start()
+
+            @pl.when(index >= 2)
+            def _():
+                self.copy(array, index - 2, False).wait()
+
+        def last_saves(self, array):
+            for index in (pieces - 2, pieces - 1):
+                self.copy(array, index, False).wait()
+
+    stage_ref = mem.stage
+    stage = Ring(stage_ref, 0)
 
     def piece_columns(index, part):
         return pl.ds(pl.multiple_of(index // CHUNKS * C_MID + part * LANES, LANES), LANES)
@@ -773,7 +888,7 @@
     ]
     for copy in feature_loads:
         copy.start()
-    first_loads(features)
+    stage.first_loads(features)
 
     padded_one, padded_two = mem.pad1, mem.pad2
     for padded in (padded_one, padded_two):
@@ -810,7 +925,7 @@
             )
         for copy in norm_out:
             copy.start()
-        advance(7)
+        hook(21)
         for copy in norm_in:
             copy.wait_recv()
         for copy in norm_out:
@@ -848,8 +963,8 @@
         width = starts[layer + 1] - starts[layer]
         mean = stats[0:1, starts[layer] : starts[layer + 1]]
         scaling = stats[1:2, starts[layer] : starts[layer + 1]]
-        outs.norm_grad[0:1, starts[layer] : starts[layer + 1]] = totals[1:2]
-        outs.norm_grad[1:2, starts[layer] : starts[layer + 1]] = totals[0:1]
+        mem.norm_grads[0:1, starts[layer] : starts[layer + 1]] = totals[1:2]
+        mem.norm_grads[1:2, starts[layer] : starts[layer + 1]] = totals[0:1]
         slope = scaling * gain(layer)
         bend = slope * scaling * totals[1:2] / count
         coef[0:1, :width] = slope
@@ -863,14 +978,6 @@
 
     zero_row = jnp.zeros((1, C_MID), f32)
 
-    def at_place(index, place, *moves):
-        if plan.inside:
-
-            @pl.when(index == place)
-            def _():
-                for move in moves:
-                    move()
-
     def column_sums(value):
         return jnp.sum(value, axis=0, keepdims=True)
 
@@ -924,20 +1031,21 @@
             right = jnp.concatenate([weights[0][:, :, :, cols].reshape(C_IN, LANES) for cols in sides], axis=1)
             put_sides(hidden_one, long_rows(0, index), sides, dot(left, right))
 
-            at_place(side * 3 + index, 1, *take(1))
-            at_place(side * 3 + index, 3, *take(1))
-
-        at_place(side, 0, lambda: cores_arrive(0))
+            hook_in(0, side * 3 + index, 6)
+
+        @pl.when(side == 0)
+        def _():
+            cores_arrive(0)
 
     sum_one = Sum(0)
     sum_one.start(row_sums[0:1, :C_MID], row_sums[1:2, :C_MID])
-    advance(1)
+    hook(1)
     sum_one.middle()
-    advance(1)
+    hook(2)
     clear_sums()
     norm_coefs(0, sum_one.finish(), row_total)
 
-    def activate(hidden_ref, slope_ref, put):
+    def activate(hidden_ref, slope_ref, put, site):
         @pl.loop(0, PIX)
         def _(pixel):
             place = pl.ds(pl.multiple_of(pixel * views, 16), views)
@@ -947,6 +1055,7 @@
                 value, slope = gelu_pair(out)
                 slope_ref[place, cols] = slope.astype(bf16)
                 put(pixel, cols, value.astype(bf16))
+            hook_in(site, pixel, SIDE, SIDE - 1, SIDE)
 
     def put_padded(padded):
         def put(pixel, cols, value):
@@ -954,8 +1063,8 @@
 
         return put
 
-    activate(hidden_one, slope_one, put_padded(padded_one))
-    advance(5)
+    activate(hidden_one, slope_one, put_padded(padded_one), 3)
+    hook(4)
 
     def patch(padded, first, count, flip):
         found = []
@@ -981,24 +1090,26 @@
         @pl.loop(0, 3)
         def _(index):
             second_part(sides, 2 * index, 2)
-            for place in range(6):
-                at_place(side * 3 + index, place, *take(1))
+            hook_in(5, side * 4 + index, 8)
 
         second_part(sides, 6, 1)
-        at_place(side, 0, lambda: cores_arrive(1))
+
+        @pl.when(side == 0)
+        def _():
+            cores_arrive(1)
 
     sum_two = Sum(1)
     sum_two.start(row_sums[0:1, :C_MID], row_sums[1:2, :C_MID])
+    hook(6)
     sum_two.middle()
-    advance(1)
+    hook(7)
     clear_sums()
     norm_coefs(1, sum_two.finish(), row_total)
 
     def put_rows(pixel, cols, value):
         act_two[pl.ds(pl.multiple_of(pixel * views, 16), views), cols] = value
 
-    activate(hidden_two, slope_two, put_rows)
-    advance(1)
+    activate(hidden_two, slope_two, put_rows, 8)
     cores_arrive(2)
 
     def weight_three(block):
@@ -1016,9 +1127,7 @@
             hidden = dot(act_two[long_rows(0, index), :], weight_three(block))
             hidden_three[long_rows(block, index), :] = hidden.astype(bf16)
             count_in(cols, hidden, hidden)
-
-        for place in range(3):
-            at_place(block, place, *take(1))
+            hook_in(9, block * 3 + index, 12)
 
         @pl.when(block == 1)
         def _():
@@ -1031,13 +1140,15 @@
     sums_high.start(row_sums[0:1, half_width:], row_sums[1:2, half_width:])
     norm_coefs(2, sums_low.finish(), row_total)
 
+    hook(22)
+
     pool, pool_slope, pool_bend = mem.pool, mem.pool_slope, mem.pool_bend
     for ref in (pool, pool_slope, pool_bend):
         ref[...] = jnp.zeros_like(ref)
 
     @pl.loop(0, pieces)
     def _(index):
-        piece_copy(features, index, True).wait()
+        stage.copy(features, index, True).wait()
 
         @pl.loop(0, C_MID // LANES)
         def _(part):
@@ -1046,7 +1157,7 @@
             slope_row, shift_row = coef[0:1, cols], coef[1:2, cols]
             kept = (pool[:, cols], pool_slope[:, cols], pool_bend[:, cols])
             for pixel in range(SIDE):
-                stage_at, hidden_at = stage_rows(index, pixel, views), hidden_rows(index, pixel, views)
+                stage_at, hidden_at = stage.rows(index, pixel, views), hidden_rows(index, pixel, views)
                 hidden = hidden_three[hidden_at, inner].astype(f32)
                 total = hidden * slope_row + shift_row + stage_ref[stage_at, inner].astype(f32)
                 value, slope = gelu_pair(total)
@@ -1054,8 +1165,8 @@
                 kept = (kept[0] + value, kept[1] + slope, kept[2] + slope * hidden)
             pool[:, cols], pool_slope[:, cols], pool_bend[:, cols] = kept
 
-        save(slope_hbm, index)
-        next_load(features, index)
+        stage.save(slope_hbm, index)
+        stage.next_load(features, index)
 
         @pl.when(index == 2)
         def _():
@@ -1065,7 +1176,9 @@
         def _():
             norm_coefs(2, sums_high.finish(), row_total, half_width)
 
-    last_saves(slope_hbm)
+        hook_in(10, index, pieces)
+
+    stage.last_saves(slope_hbm)
     cores_arrive(3)
     cores_arrive(4)
     for one in gathers:
@@ -1076,7 +1189,7 @@
     proj_hidden = dot(pooled, whole(3))
     sum_four = Sum(4)
     totals = sum_four.all(column_sums(proj_hidden), column_sums(proj_hidden * proj_hidden))
-    first_loads(slope_hbm)
+    stage.first_loads(slope_hbm)
     norm_coefs(3, totals, view_total)
     value, slope = gelu_pair(proj_hidden * coef[0:1, :P_HID] + coef[1:2, :P_HID])
     proj_act = value.astype(bf16)
@@ -1151,7 +1264,6 @@
             embed_low, proj_act[:, block * P_OUT : (block + 1) * P_OUT]
         ).astype(bf16)
     sum_four_back.middle()
-    reduces[4].core_start()
     grad_coefs(3, sum_four_back.finish(), view_total)
     four_low = (
         upstream * coef[0:1, :P_HID] - coef[1:2, :P_HID] - proj_hidden * coef[2:3, :P_HID]
@@ -1163,9 +1275,7 @@
     grad_four = dot_rows(mem.pooled[...], four_low).astype(bf16)
     weights[3][...] = grad_four.reshape(weights[3].shape)
     sum_three_back.middle()
-    four, three, two, one = reduces[3], reduces[2], reduces[1], reduces[0]
-    for place in range(plan.z):
-        four.core_start(place)
+    hook(23)
     grad_coefs(2, sum_three_back.finish(), row_total)
     pool[...] = pool_grad * coef[0:1, :]
     pool_slope[...] = pool_grad
@@ -1174,8 +1284,8 @@
 
     @pl.loop(0, pieces)
     def _(index):
-        piece_copy(slope_hbm, index, True).wait()
-        next_load(slope_hbm, index)
+        stage.copy(slope_hbm, index, True).wait()
+        stage.next_load(slope_hbm, index)
 
         @pl.loop(0, C_MID // LANES)
         def _(part):
@@ -1185,12 +1295,10 @@
             for pixel in range(SIDE):
                 hidden_at = hidden_rows(index, pixel, views)
                 hidden = hidden_three[hidden_at, inner].astype(f32)
-                slope = stage_ref[stage_rows(index, pixel, views), inner].astype(f32)
+                slope = stage_ref[stage.rows(index, pixel, views), inner].astype(f32)
                 hidden_three[hidden_at, inner] = (slope * spread - shift_row - hidden * bend_row).astype(bf16)
 
-        at_place(index, 3, reduces[4].core_add, lambda: four.core_add(0))
-        at_place(index, 11, lambda: four.core_add(1), reduces[4].first_add)
-        at_place(index, 20, lambda: four.first_add(0), lambda: four.core_add(2))
+        hook_in(11, index, pieces)
 
     @pl.loop(0, 3)
     def _(index):
@@ -1200,9 +1308,7 @@
         upstream = dot_cols(left, right) * slope_two[at, :].astype(f32)
         slope_two[at, :] = upstream.astype(bf16)
         count_in(slice(0, C_MID), upstream, hidden_two[at, :].astype(f32))
-        at_place(index, 0, lambda: four.first_add(1), lambda: four.second_add(0), reduces[4].second_add)
-        at_place(index, 1, lambda: four.core_add(3))
-        at_place(index, 2, lambda: four.first_add(2), lambda: four.second_add(1))
+        hook_in(12, index, 3)
 
     sums = row_sums[0:1, :C_MID], row_sums[1:2, :C_MID]
     sum_two_back = Sum(7)
@@ -1218,16 +1324,12 @@
         def _():
             sum_two_back.middle()
 
-        at_place(block, 0, lambda: four.first_add(3))
-        at_place(block, 2, lambda: four.second_add(2))
-        at_place(block, 3, lambda: four.second_add(3))
-
-    for place in range(plan.z):
-        three.core_start(place)
+        hook_in(13, block, BLOCKS)
+
     clear_sums()
     grad_coefs(1, sum_two_back.finish(), row_total)
 
-    def apply_grad(hidden_ref, grad_ref, put):
+    def apply_grad(hidden_ref, grad_ref, put, site):
         @pl.loop(0, PIX)
         def _(pixel):
             place = pl.ds(pl.multiple_of(pixel * views, 16), views)
@@ -1239,9 +1341,9 @@
                     - hidden_ref[place, cols].astype(f32) * coef[2:3, cols]
                 )
                 put(pixel, cols, grad.astype(bf16))
-
-    apply_grad(hidden_two, slope_two, put_padded(padded_two))
-    reduces[4].finish()
+            hook_in(site, pixel, SIDE, SIDE - 1, SIDE)
+
+    apply_grad(hidden_two, slope_two, put_padded(padded_two), 14)
     column_places = [
         hidden_three.at[pl.ds(2 * rows, rows)],
         hidden_three.at[pl.ds(3 * rows, rows)],
@@ -1251,9 +1353,6 @@
     column_loads = [feature_copy(block, column_places[block]) for block in range(BLOCKS)]
     for copy in column_loads:
         copy.start()
-    three.core_add(0)
-    three.core_add(1)
-
     def tap_grad(tap):
         down, across = tap // 3, tap % 3
         left = padded_one[pl.ds(down, SIDE), pl.ds(pl.multiple_of(across * views, 16), chunk), :]
@@ -1261,23 +1360,10 @@
         grad = dot_rows(left.reshape(rows, C_MID), right.reshape(rows, C_MID))
         stage_ref[pl.ds(pl.multiple_of(tap * C_MID, 16), C_MID), :] = grad.astype(bf16)
 
-    pl.loop(0, 3)(tap_grad)
-    two.core_start(0)
-    three.first_add(0)
-    three.core_add(2)
-    three.core_add(3)
-    pl.loop(3, 5)(tap_grad)
-    two.core_start(1)
-    two.core_add(0)
-    three.first_add(1)
-    three.second_add(0)
-    pl.loop(5, 7)(tap_grad)
-    two.core_start(2)
-    three.first_add(2)
-    three.first_add(3)
-    two.core_add(1)
-    three.second_add(1)
-    four.finish()
+    @pl.loop(0, 7)
+    def _(tap):
+        tap_grad(tap)
+        hook_in(15, tap, 7)
 
     def second_back(first, count):
         flat = weights[1][...].reshape(9 * C_MID, C_MID)
@@ -1290,13 +1376,10 @@
     @pl.loop(0, 3)
     def _(index):
         second_back(2 * index, 2)
-        at_place(
-            index, 0, lambda: two.first_add(0), lambda: two.core_add(2), lambda: three.second_add(2), lambda: three.second_add(3)
-        )
-        at_place(index, 1, lambda: two.first_add(1), three.finish, lambda: two.second_add(0))
-        at_place(index, 2, lambda: two.first_add(2), lambda: two.second_add(1))
+        hook_in(16, index, 3)
 
     second_back(6, 1)
+    hook(16, 3)
     sums = row_sums[0:1, :C_MID], row_sums[1:2, :C_MID]
     sum_one_back = Sum(8)
     sum_one_back.start(sums[0], xhat_sum(0, *sums))
@@ -1309,40 +1392,27 @@
         def _():
             sum_one_back.middle()
 
-    two.core_start(3)
-    two.second_add(2)
+        hook_in(17, tap, 2, 7)
+
     grad_coefs(0, sum_one_back.finish(), row_total)
 
     def put_one(pixel, cols, value):
         act_two[pl.ds(pl.multiple_of(pixel * views, 16), views), cols] = value
 
-    apply_grad(hidden_one, slope_one, put_one)
-    two.core_add(3)
+    apply_grad(hidden_one, slope_one, put_one, 18)
 
     def block_grad(block):
         column_loads[block].wait()
         grad = dot_rows(column_places[block][...], act_two[...])
         mem.g1[block] = grad.astype(bf16).reshape(plan.x, -1, C_MID)
 
-    block_grad(0)
-    one.core_start(0)
-    two.first_add(3)
-    block_grad(1)
-    one.core_start(1)
-    one.core_add(0)
-    two.second_add(3)
-    block_grad(2)
-    one.core_start(2)
-    one.core_add(1)
-    one.first_add(0)
-    block_grad(3)
-    one.core_start(3)
-    one.core_add(2)
-    one.first_add(1)
-    one.second_add(0)
-    two.finish()
-
-    first_loads(slope_hbm)
+    tail = Ring(hidden_three, 2 * rows)
+    for block in range(BLOCKS):
+        block_grad(block)
+        hook(19, block)
+        if block == 1:
+            tail.first_loads(slope_hbm)
+
     sum_last = Sum(9)
 
     @pl.loop(0, pieces)
@@ -1350,32 +1420,45 @@
         block = index // CHUNKS
         weight = weights[0][block].reshape(C_MID, C_MID)
         back = dot_cols(act_two[span(lax.rem(index, CHUNKS)), :], weight)
-        piece_copy(slope_hbm, index, True).wait()
+        tail.copy(slope_hbm, index, True).wait()
         cols = pl.ds(pl.multiple_of(block * C_MID, LANES), C_MID)
         for pixel in range(SIDE):
-            at = stage_rows(index, pixel, views)
-            summed = stage_ref[at, :].astype(f32) * pool_slope[:, cols]
-            stage_ref[at, :] = (summed + back[pixel * views : (pixel + 1) * views]).astype(bf16)
-        save(outs.features_grad, index)
-        next_load(slope_hbm, index)
-        at_place(index, 2, lambda: one.core_add(3), lambda: one.first_add(2), lambda: one.second_add(1))
-        at_place(index, 8, lambda: one.first_add(3), lambda: one.second_add(2))
-        at_place(index, 13, lambda: one.second_add(3))
-        at_place(index, 20, one.finish, lambda: sum_last.start(mem.squares[...], mem.squares[...]))
-        at_place(index, 24, sum_last.middle)
-
-    last_saves(outs.features_grad)
+            at = tail.rows(index, pixel, views)
+            summed = hidden_three[at, :].astype(f32) * pool_slope[:, cols]
+            hidden_three[at, :] = (summed + back[pixel * views : (pixel + 1) * views]).astype(bf16)
+        tail.save(outs.features_grad, index)
+        tail.next_load(slope_hbm, index)
+        hook_in(20, index, pieces)
+        if plan.inside:
+
+            @pl.when(index == LAST_SUM)
+            def _():
+                sum_last.start(mem.squares[...], mem.squares[...])
+
+            @pl.when(index == LAST_SUM + 3)
+            def _():
+                sum_last.middle()
+
+    tail.last_saves(outs.features_grad)
     squares = mem.squares[...]
     if plan.inside:
         squares = sum_last.finish()[0:1]
-    norm_grads = outs.norm_grad[...]
+    norm_grads = mem.norm_grads[...]
     scalars = outs.scalars
     norm_squares = column_sums(norm_grads * norm_grads)
     for place in range(norm_squares.shape[1] // LANES):
         squares = squares + norm_squares[:, place * LANES : (place + 1) * LANES]
     scalars[...] = jnp.zeros_like(scalars)
-    scalars[0:1, :] = jnp.broadcast_to(jnp.sum(objective_row, axis=1, keepdims=True) / image_total, (1, LANES))
-    scalars[1:2, :] = jnp.broadcast_to(jnp.sum(squares, axis=1, keepdims=True), (1, LANES))
+    squares = jnp.sum(squares, axis=1, keepdims=True)
+    norm = jnp.sqrt(squares)
+    found = (jnp.sum(objective_row, axis=1, keepdims=True) / image_total, squares, norm, clip_factor(norm))
+    for place, value in enumerate(found):
+        scalars[place : place + 1, :] = jnp.broadcast_to(value, (1, LANES))
+    if plan.inside:
+        owner = (dp_me * plan.fsdp + fsdp_me) * LANES
+        outs.norm_grad[...] = mem.norm_grads[:, pl.ds(pl.multiple_of(owner, LANES), LANES)]
+    else:
+        outs.norm_grad[...] = norm_grads
     if not plan.inside:
         stores = [
             pltpu.make_async_copy(gradients[which], outs.grads[which], mem.bulk_send.at[which])
@@ -1407,7 +1490,7 @@
     results = [
         ((rows, C_IN), bf16, anywhere),
         ((rows, C_IN), bf16, anywhere),
-        ((2, norm_width()), f32, in_vmem),
+        (norm.shape, f32, in_vmem),
         ((8, LANES), f32, in_vmem),
     ]
     for which, shard in enumerate(shards):
@@ -1470,6 +1553,7 @@
         coef=pltpu.VMEM((8, C_IN), f32),
         stats=pltpu.VMEM((2, norm_width()), f32),
         norm=pltpu.VMEM((2, norm_width()), f32),
+        norm_grads=pltpu.VMEM((2, norm_width()), f32),
         norm_tiles=pltpu.VMEM((plan.dp, plan.fsdp, 2, LANES), f32),
         norm_s0=dma((plan.dp,)),
         norm_r0=dma((plan.dp,)),
@@ -1502,6 +1586,10 @@
     return 2 * C_MID + C_IN + P_HID
 
 
+def clip_factor(norm):
+    return clip_level / jnp.maximum(norm, clip_level)
+
+
 def adam_update(weight, moment_one, moment_two, gradient, step_rate, weight_decay):
     first_new = beta_first * moment_one + (1.0 - beta_first) * gradient
     second_new = beta_second * moment_two + (1.0 - beta_second) * gradient * gradient
@@ -1515,42 +1603,47 @@
 
 def finish_kernel(rates, decays, *refs):
     count = len(rates)
-    low, factor = refs[0], refs[1]
+    low, scalars = refs[0], refs[1]
     given, results = refs[2 : 2 + 4 * count], refs[2 + 4 * count :]
     results[0][...] = low[...].astype(f32)
 
     @pl.when(pl.program_id(0) == 0)
     def _():
-        scale = factor[0, 0]
+        results[1][0, 0] = scalars[0, 0]
+        results[2][0, 0] = scalars[2, 0]
+        scale = scalars[3, 0]
         for place in range(count):
             weight, first, second, grad = (given[part * count + place][...] for part in range(4))
             updated = adam_update(weight, first, second, grad * scale, rates[place], decays[place])
             for part in range(3):
-                results[1 + part * count + place][...] = updated[part]
-
-
-def finish(features_grad, factor, masters, firsts, seconds, grads, rates, decays):
+                results[3 + part * count + place][...] = updated[part]
+
+
+def finish(features_grad, scalars, masters, firsts, seconds, grads, rates, decays):
     rows = features_grad.shape[0]
     arrays = [*masters, *firsts, *seconds, *grads]
 
     def fixed(shape):
         return pl.BlockSpec(shape, lambda index: (0, 0))
 
-    step = rows // CHUNKS
-    moving = pl.BlockSpec((step, C_IN), lambda index: (index, 0))
+    steps = 2 * CHUNKS
+    moving = pl.BlockSpec((rows // steps, C_IN), lambda index: (index, 0))
+    single = pl.BlockSpec(memory_space=pltpu.SMEM)
     outputs = [*masters] * 3
     values = pl.pallas_call(
         lambda *refs: finish_kernel(rates, decays, *refs),
-        grid=(CHUNKS,),
-        in_specs=[moving, pl.BlockSpec(memory_space=pltpu.SMEM)] + [fixed(array.shape) for array in arrays],
-        out_specs=[moving] + [fixed(array.shape) for array in outputs],
+        grid=(steps,),
+        in_specs=[moving, single] + [fixed(array.shape) for array in arrays],
+        out_specs=[moving, single, single] + [fixed(array.shape) for array in outputs],
         out_shape=[jax.ShapeDtypeStruct((rows, C_IN), f32)]
+        + [jax.ShapeDtypeStruct((1, 1), f32)] * 2
         + [jax.ShapeDtypeStruct(array.shape, f32) for array in outputs],
         compiler_params=pltpu.CompilerParams(vmem_limit_bytes=62 * 2**20),
         name="finish",
-    )(features_grad, factor, *arrays)
+    )(features_grad, scalars, *arrays)
     count = len(masters)
-    return values[0], values[1 : 1 + count], values[1 + count : 1 + 2 * count], values[1 + 2 * count :]
+    groups = [values[3 + part * count : 3 + (part + 1) * count] for part in range(3)]
+    return values[0], values[1].reshape(()), values[2].reshape(()), *groups
 
 
 def gather_full(weight):
@@ -1587,7 +1680,7 @@
         norm = lax.all_gather(norm_params.astype(bf16), (DP, FSDP), axis=1, tiled=True).astype(f32)
     got = run_kernel(plan, pixels, view_order, shards, norm)
     grads = list(got.grads)
-    squares = got.scalars[1, 0]
+    scalars = got.scalars
     turned = [list(group) for group in (masters, firsts, seconds)]
     if inside:
         owned = grads
@@ -1602,12 +1695,15 @@
             grads[4].swapaxes(2, 3).reshape(P_HID, P_OUT),
         ]
         owned = [scatter_full(gradient) for gradient in whole_grads]
-        squares = squares + lax.psum(sum(jnp.sum(grad * grad) for grad in owned), (DP, FSDP))
+        squares = scalars[1, 0] + lax.psum(sum(jnp.sum(grad * grad) for grad in owned), (DP, FSDP))
+        norm_value = jnp.sqrt(squares)
+        scalars = scalars.at[2].set(norm_value).at[3].set(clip_factor(norm_value))
     width = norm_params.shape[1]
-    owner = lax.axis_index((DP, FSDP))
-    owned.append(lax.dynamic_slice_in_dim(got.norm_grad, owner * width, width, 1))
-    grad_norm = jnp.sqrt(squares)
-    factor = clip_level / jnp.maximum(grad_norm, clip_level)
+    if inside:
+        owned.append(got.norm_grad)
+    else:
+        owner = lax.axis_index((DP, FSDP))
+        owned.append(lax.dynamic_slice_in_dim(got.norm_grad, owner * width, width, 1))
     step_rates = (
         C_IN ** (-0.5),
         (9 * C_MID) ** (-0.5),
@@ -1617,13 +1713,13 @@
         norm_rate,
     )
     decays = (decay_rate, decay_rate, decay_rate, decay_rate, decay_rate, 0.0)
-    input_grad, *updates = finish(
-        got.features_grad, factor.reshape(1, 1), *turned, owned, step_rates, decays
+    input_grad, loss, grad_norm, *updates = finish(
+        got.features_grad, scalars, *turned, owned, step_rates, decays
     )
     if inside:
         updates = [[*group[:4], group[4].T, group[5]] for group in updates]
     return (
-        got.scalars[0, 0],
+        loss,
         jnp.swapaxes(input_grad.reshape(PIX, views, C_IN), 0, 1),
         grad_norm,
         *updates[0],

time: 305 us -> 310 us (1.016)
  Pallas kernels: 300 us -> 308 us
    pallas_call x1, Pallas kernels: 286 us -> 292 us  [run_kernel(): pl.pallas_call(lambda *refs: kernel(plan, *refs), out_shape=[jax.ShapeDty...]
where the time goes in v1:
time: 310 us; the launch traced here: 309 us
  Pallas kernels  308 us (99%)
    pallas_call x1, Pallas kernels, run_kernel(): pl.pallas_call(lambda *refs: kernel(plan, *refs), out_shape=[jax.ShapeDty...  292 us
    pallas_call x1, Pallas kernels, finish(): pl.pallas_call(lambda *refs: finish_kernel(rates, decays, *refs), grid=(s...  16.8 us

profile of v1, /device:TPU:0, one launch (start us, length us, event | category | flops | bytes accessed | tf_op | source)
XLA Modules:
  0.0 309.3 jit_solution(7999239757934156349)
XLA Ops:
  0.7 291.7 %train_step.1 = (bf16[2352,2048]{1,0:T(8,128)(2,1)}, bf16[2352,2048]{1,0:T(8,128)(2,1)}, f32[2,128]{1,0:T(2,128)}, f32[8,128]{1,0:T(8,128)}, f32[256,128]{1,0:T(...) custom-call(bf16[2352,2048]{1,0:T(8,128)(2,1)} %bitcast.14, ...), custom_call_target="tpu_custom_call" | custom-call | tf_op jit(solution)/shard_map/train_step/pallas_call | solution.py:1571
  292.4 16.8 %finish.1 = (f32[2352,2048]{1,0:T(8,128)}, f32[1,1]{1,0:T(1,128)}, f32[1,1]{1,0:T(1,128)}, f32[256,128]{1,0:T(8,128)}, f32[576,128]{1,0:T(8,128)}, /*index=5*/f3...) custom-call(bf16[2352,2048]{1,0:T(8,128)(2,1)} %get-tuple-element.50, ...), custom_call_target="tpu_custom_call" | custom-call | tf_op jit(solution)/shard_map/finish/pallas_call | solution.py:1633

commit v2 on v1

--- a/solution.py
+++ b/solution.py
@@ -19,6 +19,7 @@
 CHUNKS = SIDE
 SLOTS = 6
 LAST_SUM = 23
+COPIES = 360
 
 
 highest = lax.Precision.HIGHEST
@@ -136,69 +137,49 @@
     (0, 1): 1,
     (0, 3): 1,
     (1, 0): 1,
-    (3, 0): 1,
-    (3, 2): 1,
-    (3, 3): 1,
-    (3, 6): 1,
+    (2, 0): 1,
+    (4, 0): 5,
+    (5, 0): 1,
     (5, 1): 1,
+    (5, 2): 1,
     (5, 4): 1,
-    (6, 0): 2,
-    (9, 4): 1,
-    (9, 11): 1,
-    (10, 0): 1,
-    (10, 7): 1,
-    (10, 15): 2,
-    (10, 21): 1,
-    (21, 0): 9,
+    (5, 5): 1,
+    (5, 6): 1,
+    (7, 0): 1,
+    (8, 6): 1,
+    (9, 2): 1,
+    (9, 5): 1,
+    (9, 8): 1,
+    (21, 0): 7,
 }
 REDUCE_AT = {
-    (11, 0): ((4, 0, 0),),
-    (11, 6): ((3, 2, 0),),
-    (11, 7): ((3, 3, 0),),
-    (11, 13): ((3, 0, 0),),
-    (11, 17): ((3, 1, 1),),
-    (11, 21): ((4, 0, 1),),
-    (11, 25): ((3, 2, 1),),
-    (12, 2): ((3, 3, 1), (3, 1, 2)),
-    (13, 2): ((3, 0, 1),),
-    (13, 3): ((2, 0, 0),),
-    (14, 1): ((3, 2, 2),),
-    (14, 2): ((3, 3, 2),),
-    (14, 4): ((3, 1, 3), (2, 2, 0)),
-    (14, 6): ((2, 3, 0), (2, 1, 0)),
-    (15, 0): ((2, 0, 1),),
-    (15, 1): ((3, 0, 2),),
-    (15, 2): ((4, 0, 2),),
-    (15, 3): ((2, 3, 1),),
-    (15, 4): ((1, 1, 0),),
-    (15, 5): ((1, 0, 0), (2, 2, 1), (2, 1, 1)),
-    (15, 6): ((3, 3, 3), (3, 2, 3)),
-    (16, 0): ((2, 0, 2), (2, 2, 2), (1, 1, 1), (1, 2, 0)),
-    (16, 1): ((3, 0, 3), (2, 1, 2), (1, 0, 1)),
-    (16, 2): ((2, 3, 2),),
-    (16, 3): ((3, 9, 4), (2, 0, 3), (1, 2, 1)),
-    (17, 0): ((2, 1, 3),),
-    (17, 1): ((1, 3, 0), (1, 0, 2), (2, 3, 3), (2, 2, 3)),
-    (18, 0): ((1, 1, 2),),
-    (18, 4): ((4, 0, 3),),
-    (18, 5): ((1, 3, 1),),
-    (19, 0): ((2, 9, 4), (1, 0, 3), (1, 1, 3), (1, 2, 2)),
-    (19, 1): ((0, 1, 0), (0, 0, 0), (1, 3, 2)),
-    (19, 2): ((1, 2, 3), (0, 1, 1), (0, 2, 0)),
-    (19, 3): ((0, 0, 1),),
-    (20, 0): ((0, 3, 0),),
-    (20, 2): ((0, 2, 1),),
-    (20, 4): ((0, 1, 2), (1, 3, 3)),
-    (20, 6): ((0, 3, 1),),
-    (20, 8): ((0, 2, 2),),
-    (20, 10): ((0, 0, 2), (0, 1, 3)),
-    (20, 12): ((4, 9, 4),),
-    (20, 13): ((0, 3, 2),),
-    (20, 14): ((0, 2, 3),),
-    (20, 17): ((0, 0, 3), (1, 9, 4)),
-    (20, 18): ((0, 3, 3),),
-    (20, 22): ((0, 9, 4),),
-    (23, 0): ((3, 1, 0),),
+    (11, 3): ((4, 0, 1), (3, 0, 1)),
+    (11, 11): ((3, 1, 1), (4, 0, 2)),
+    (11, 20): ((3, 0, 2), (3, 2, 1)),
+    (12, 0): ((3, 1, 2), (3, 0, 3), (4, 0, 3)),
+    (12, 1): ((3, 3, 1),),
+    (12, 2): ((3, 2, 2), (3, 1, 3)),
+    (13, 0): ((3, 3, 2),),
+    (13, 2): ((3, 2, 3),),
+    (13, 3): ((3, 3, 3), (2, 0, 0), (2, 1, 0), (2, 2, 0), (2, 3, 0)),
+    (14, 6): ((4, 9, 4), (2, 0, 1), (2, 1, 1)),
+    (15, 2): ((1, 0, 0), (2, 0, 2), (2, 2, 1), (2, 3, 1)),
+    (15, 4): ((1, 1, 0), (1, 0, 1), (2, 1, 2), (2, 0, 3)),
+    (15, 6): ((1, 2, 0), (2, 2, 2), (2, 3, 2), (1, 1, 1), (2, 1, 3), (3, 9, 4)),
+    (16, 0): ((1, 0, 2), (1, 2, 1), (2, 2, 3), (2, 3, 3)),
+    (16, 1): ((1, 1, 2), (2, 9, 4), (1, 0, 3)),
+    (16, 2): ((1, 2, 2), (1, 1, 3)),
+    (17, 1): ((1, 3, 0), (1, 2, 3)),
+    (18, 6): ((1, 3, 1),),
+    (19, 0): ((0, 0, 0), (1, 3, 2)),
+    (19, 1): ((0, 1, 0), (0, 0, 1), (1, 3, 3)),
+    (19, 2): ((0, 2, 0), (0, 1, 1), (0, 0, 2)),
+    (19, 3): ((0, 3, 0), (0, 2, 1), (0, 1, 2), (0, 0, 3), (1, 9, 4)),
+    (20, 2): ((0, 3, 1), (0, 2, 2), (0, 1, 3)),
+    (20, 8): ((0, 3, 2), (0, 2, 3)),
+    (20, 13): ((0, 3, 3),),
+    (20, 20): ((0, 9, 4),),
+    (23, 0): ((4, 0, 0), (3, 0, 0), (3, 1, 0), (3, 2, 0), (3, 3, 0)),
 }
 
 
@@ -554,8 +535,9 @@
             self.which, self.rows = which, (start, size)
             both, low, high = (start, size), (start, size // 2), (start + size // 2, size // 2)
 
-            def at(*index):
-                return pick(ref, places(which, *index, False))
+            def at(z_index, *index):
+                found = [slice(0, 2), slice(2, 4)] if z_index is None else [z_index]
+                return [one for z_one in found for one in pick(ref, places(which, z_one, *index, False))]
 
             own = at(z_me, x_me, dp_me, both)[0]
             self.line = LineBatch(
@@ -802,6 +784,7 @@
 
     gradients = [mem.g1, mem.stage.at[pl.ds(0, 9 * C_MID)], weights[2], weights[3], weights[4]]
     reduces = [Reduce(which, gradients[which], which < 4) for which in range(5)]
+    assert counter[0] <= COPIES
     mem.squares[...] = jnp.zeros((1, LANES), f32)
 
     if plan.inside:
@@ -1559,8 +1542,8 @@
         norm_r0=dma((plan.dp,)),
         norm_s1=dma((plan.fsdp,)),
         norm_r1=dma((plan.fsdp,)),
-        bulk_send=dma((300,)),
-        bulk_recv=dma((300,)),
+        bulk_send=dma((COPIES,)),
+        bulk_recv=dma((COPIES,)),
         mats=[matrix_room(), matrix_room()],
         sums=[
             sum_room(width)
@@ -1604,44 +1587,65 @@
 def finish_kernel(rates, decays, *refs):
     count = len(rates)
     low, scalars = refs[0], refs[1]
-    given, results = refs[2 : 2 + 4 * count], refs[2 + 4 * count :]
-    results[0][...] = low[...].astype(f32)
-
-    @pl.when(pl.program_id(0) == 0)
+    refs = refs[2:]
+    given, wide, loss, norm, updated = refs[: 4 * count], *refs[4 * count : 4 * count + 3], refs[4 * count + 3 : -2]
+    rooms, sems = refs[-2], refs[-1]
+    wide[...] = low[...].astype(f32)
+    step = pl.program_id(0)
+
+    def load(place):
+        return pltpu.make_async_copy(given[place], rooms[place], sems.at[place])
+
+    def store(place):
+        return pltpu.make_async_copy(rooms[place], updated[place], sems.at[place])
+
+    @pl.when(step == 0)
     def _():
-        results[1][0, 0] = scalars[0, 0]
-        results[2][0, 0] = scalars[2, 0]
-        scale = scalars[3, 0]
+        loss[0, 0] = scalars[0, 0]
+        norm[0, 0] = scalars[2, 0]
+        for place in range(4 * count):
+            load(place).start()
+
+    @pl.when(step == 2)
+    def _():
+        for place in range(4 * count):
+            load(place).wait()
         for place in range(count):
-            weight, first, second, grad = (given[part * count + place][...] for part in range(4))
-            updated = adam_update(weight, first, second, grad * scale, rates[place], decays[place])
+            weight, first, second, grad = (rooms[part * count + place][...] for part in range(4))
+            found = adam_update(weight, first, second, grad * scalars[3, 0], rates[place], decays[place])
             for part in range(3):
-                results[3 + part * count + place][...] = updated[part]
+                rooms[part * count + place][...] = found[part]
+        for place in range(3 * count):
+            store(place).start()
+
+    @pl.when(step == CHUNKS - 1)
+    def _():
+        for place in range(3 * count):
+            store(place).wait()
 
 
 def finish(features_grad, scalars, masters, firsts, seconds, grads, rates, decays):
     rows = features_grad.shape[0]
     arrays = [*masters, *firsts, *seconds, *grads]
-
-    def fixed(shape):
-        return pl.BlockSpec(shape, lambda index: (0, 0))
-
-    steps = 2 * CHUNKS
-    moving = pl.BlockSpec((rows // steps, C_IN), lambda index: (index, 0))
+    moving = pl.BlockSpec((rows // CHUNKS, C_IN), lambda index: (index, 0))
     single = pl.BlockSpec(memory_space=pltpu.SMEM)
-    outputs = [*masters] * 3
+    anywhere = pl.BlockSpec(memory_space=pl.ANY)
+    count = len(masters)
     values = pl.pallas_call(
         lambda *refs: finish_kernel(rates, decays, *refs),
-        grid=(steps,),
-        in_specs=[moving, single] + [fixed(array.shape) for array in arrays],
-        out_specs=[moving, single, single] + [fixed(array.shape) for array in outputs],
+        grid=(CHUNKS,),
+        in_specs=[moving, single] + [anywhere] * (4 * count),
+        out_specs=[moving, single, single] + [anywhere] * (3 * count),
         out_shape=[jax.ShapeDtypeStruct((rows, C_IN), f32)]
         + [jax.ShapeDtypeStruct((1, 1), f32)] * 2
-        + [jax.ShapeDtypeStruct(array.shape, f32) for array in outputs],
+        + [jax.ShapeDtypeStruct(array.shape, f32) for array in arrays[: 3 * count]],
+        scratch_shapes=[
+            [pltpu.VMEM(array.shape, f32) for array in arrays],
+            pltpu.SemaphoreType.DMA((4 * count,)),
+        ],
         compiler_params=pltpu.CompilerParams(vmem_limit_bytes=62 * 2**20),
         name="finish",
     )(features_grad, scalars, *arrays)
-    count = len(masters)
     groups = [values[3 + part * count : 3 + (part + 1) * count] for part in range(3)]
     return values[0], values[1].reshape(()), values[2].reshape(()), *groups
 

time: 310 us -> 307 us (level)
  no operation moved by 1% of the time
where the time goes in v2:
time: 307 us; the launch traced here: 306 us
  Pallas kernels  305 us (99%)
    pallas_call x1, Pallas kernels, run_kernel(): pl.pallas_call(lambda *refs: kernel(plan, *refs), out_shape=[jax.ShapeDty...  291 us
    pallas_call x1, Pallas kernels, finish(): pl.pallas_call(lambda *refs: finish_kernel(rates, decays, *refs), grid=(C...  14.6 us

profile of v2, /device:TPU:0, one launch (start us, length us, event | category | flops | bytes accessed | tf_op | source)
XLA Modules:
  0.0 306.3 jit_solution(1769148462626889538)
XLA Ops:
  0.7 290.9 %train_step.1 = (bf16[2352,2048]{1,0:T(8,128)(2,1)}, bf16[2352,2048]{1,0:T(8,128)(2,1)}, f32[2,128]{1,0:T(2,128)}, f32[8,128]{1,0:T(8,128)}, f32[256,128]{1,0:T(...) custom-call(bf16[2352,2048]{1,0:T(8,128)(2,1)} %bitcast.14, ...), custom_call_target="tpu_custom_call" | custom-call | tf_op jit(solution)/shard_map/train_step/pallas_call | solution.py:1554
  291.6 14.6 %finish.1 = (f32[2352,2048]{1,0:T(8,128)}, f32[1,1]{1,0:T(1,128)}, f32[1,1]{1,0:T(1,128)}, f32[256,128]{1,0:T(8,128)}, f32[576,128]{1,0:T(8,128)}, /*index=5*/f3...) custom-call(bf16[2352,2048]{1,0:T(8,128)(2,1)} %get-tuple-element.50, ...), custom_call_target="tpu_custom_call" | custom-call | tf_op jit(solution)/shard_map/finish/pallas_call | solution.py:1634

commit v3 on v2

--- a/solution.py
+++ b/solution.py
@@ -268,6 +268,7 @@
         self.devices = dp_size * fsdp_size
         self.views = views
         self.rows = views * PIX
+        self.tall = -(-self.rows // C_MID) * C_MID
         self.chunk = views * SIDE
         self.inside = inside
         self.z = 4
@@ -280,7 +281,7 @@
 
 def kernel(plan, *refs):
     ins, outs, mem = Ins(*refs[:3], refs[3:8]), Outs(*refs[8:12], refs[12:17]), refs[17]
-    views, chunk, rows = plan.views, plan.chunk, plan.rows
+    views, chunk, rows, tall = plan.views, plan.chunk, plan.rows, plan.tall
     row_total = float(rows * plan.devices)
     view_total = float(views * plan.devices)
     image_total = float(views * plan.devices // 2)
@@ -535,9 +536,8 @@
             self.which, self.rows = which, (start, size)
             both, low, high = (start, size), (start, size // 2), (start + size // 2, size // 2)
 
-            def at(z_index, *index):
-                found = [slice(0, 2), slice(2, 4)] if z_index is None else [z_index]
-                return [one for z_one in found for one in pick(ref, places(which, z_one, *index, False))]
+            def at(*index):
+                return pick(ref, places(which, *index, False))
 
             own = at(z_me, x_me, dp_me, both)[0]
             self.line = LineBatch(
@@ -879,6 +879,9 @@
             padded[edge] = jnp.zeros((padded.shape[1], C_MID), bf16)
         for edge in (0, SIDE + 1):
             padded[:, pl.ds(edge * views, views), :] = jnp.zeros((SIDE + 2, views, C_MID), bf16)
+    rest = jnp.zeros((tall - rows, C_MID), bf16)
+    for ref, end in ((mem.d1, rows), (mem.h2, rows), (mem.d2, rows), (mem.a2, rows), (hidden_three, BLOCKS * rows)):
+        ref[end : end + tall - rows, :] = rest
 
     if plan.inside:
         norm_dp[1]()
@@ -983,6 +986,40 @@
             pl.ds(pl.multiple_of(half * (C_MID // 2) + core * LANES, LANES), LANES) for half in range(2)
         ]
 
+    def turn_rows(ref):
+        @pl.loop(0, tall // C_MID)
+        def _(block):
+            at = pl.ds(pl.multiple_of(block * C_MID, C_MID), C_MID)
+            ref[at, :] = ref[at, :].T
+
+    def turned(ref):
+        return jnp.concatenate([ref[start : start + C_MID, :] for start in range(0, tall, C_MID)], axis=1)
+
+    def sends_leave(which):
+        for one in gathers:
+            if one.which == which:
+                one.leave()
+
+    def turn_weight(which, block):
+        ref = weights[which]
+        if which == 1:
+            groups = [block * 8 + group for group in range(8)]
+            ats = [
+                (group // 18, group // 9 % 2, pl.ds(pl.multiple_of(group % 9 * 64, 64), 64), everything)
+                for group in groups
+            ]
+            value = jnp.concatenate([ref[at] for at in ats], axis=0).T
+            for place, at in enumerate(ats):
+                ref[at] = value[place * 64 : (place + 1) * 64, :]
+        elif which == 3:
+            for half in range(P_HID // C_MID):
+                cols = slice(half * C_MID, (half + 1) * C_MID)
+                value = ref[block, :, :, cols]
+                ref[block, :, :, cols] = value.reshape(C_MID, C_MID).T.reshape(value.shape)
+        else:
+            value = ref[block]
+            ref[block] = value.reshape(C_MID, C_MID).T.reshape(value.shape)
+
     hidden_one, slope_one = mem.h1, mem.d1
     hidden_two, slope_two = mem.h2, mem.d2
     act_two = mem.a2
@@ -1023,7 +1060,10 @@
     sum_one = Sum(0)
     sum_one.start(row_sums[0:1, :C_MID], row_sums[1:2, :C_MID])
     hook(1)
+    sends_leave(0)
+    pl.loop(0, 2)(lambda block: turn_weight(0, block))
     sum_one.middle()
+    pl.loop(2, 4)(lambda block: turn_weight(0, block))
     hook(2)
     clear_sums()
     norm_coefs(0, sum_one.finish(), row_total)
@@ -1084,7 +1124,10 @@
     sum_two = Sum(1)
     sum_two.start(row_sums[0:1, :C_MID], row_sums[1:2, :C_MID])
     hook(6)
+    sends_leave(1)
+    pl.loop(0, 4)(lambda block: turn_weight(1, block))
     sum_two.middle()
+    pl.loop(4, 9)(lambda block: turn_weight(1, block))
     hook(7)
     clear_sums()
     norm_coefs(1, sum_two.finish(), row_total)
@@ -1164,14 +1207,18 @@
     stage.last_saves(slope_hbm)
     cores_arrive(3)
     cores_arrive(4)
-    for one in gathers:
-        one.leave()
+    for which in range(2, 5):
+        sends_leave(which)
 
     pooled = (pool[...] * (1.0 / PIX)).astype(bf16)
     mem.pooled[...] = pooled
     proj_hidden = dot(pooled, whole(3))
     sum_four = Sum(4)
-    totals = sum_four.all(column_sums(proj_hidden), column_sums(proj_hidden * proj_hidden))
+    sum_four.start(column_sums(proj_hidden), column_sums(proj_hidden * proj_hidden))
+    pl.loop(0, 2)(lambda block: turn_weight(3, block))
+    sum_four.middle()
+    pl.loop(2, 4)(lambda block: turn_weight(3, block))
+    totals = sum_four.finish()
     stage.first_loads(slope_hbm)
     norm_coefs(3, totals, view_total)
     value, slope = gelu_pair(proj_hidden * coef[0:1, :P_HID] + coef[1:2, :P_HID])
@@ -1246,22 +1293,37 @@
         weights[4][block // plan.x, block % plan.x] = dot_rows(
             embed_low, proj_act[:, block * P_OUT : (block + 1) * P_OUT]
         ).astype(bf16)
+    pl.loop(0, 4)(lambda block: turn_weight(2, block))
     sum_four_back.middle()
+    turn_rows(act_two)
     grad_coefs(3, sum_four_back.finish(), view_total)
     four_low = (
         upstream * coef[0:1, :P_HID] - coef[1:2, :P_HID] - proj_hidden * coef[2:3, :P_HID]
     ).astype(bf16)
-    pool_grad = dot_cols(four_low, whole(3)) * (1.0 / PIX)
-    plain = column_sums(pool_grad * pool_slope[...])
+    @pl.loop(0, BLOCKS)
+    def _(block):
+        cols = pl.ds(pl.multiple_of(block * C_MID, LANES), C_MID)
+        right = jnp.concatenate(
+            [
+                weights[3][block, :, :, half * C_MID : (half + 1) * C_MID].reshape(C_MID, C_MID)
+                for half in range(P_HID // C_MID)
+            ],
+            axis=0,
+        )
+        grad = dot(four_low, right) * (1.0 / PIX)
+        row_sums[0:1, cols] = column_sums(grad * pool_slope[:, cols])
+        row_sums[1:2, cols] = column_sums(grad * pool_bend[:, cols])
+        pool_slope[:, cols] = grad
+
+    plain = row_sums[0:1, :]
     sum_three_back = Sum(6)
-    sum_three_back.start(plain, xhat_sum(2, plain, column_sums(pool_grad * pool_bend[...])))
+    sum_three_back.start(plain, xhat_sum(2, plain, row_sums[1:2, :]))
     grad_four = dot_rows(mem.pooled[...], four_low).astype(bf16)
     weights[3][...] = grad_four.reshape(weights[3].shape)
     sum_three_back.middle()
     hook(23)
     grad_coefs(2, sum_three_back.finish(), row_total)
-    pool[...] = pool_grad * coef[0:1, :]
-    pool_slope[...] = pool_grad
+    pool[...] = pool_slope[...] * coef[0:1, :]
 
     clear_sums()
 
@@ -1287,8 +1349,7 @@
     def _(index):
         at = long_rows(0, index)
         left = jnp.concatenate([hidden_three[long_rows(block, index), :] for block in range(BLOCKS)], axis=1)
-        right = jnp.concatenate([weight_three(block) for block in range(BLOCKS)], axis=1)
-        upstream = dot_cols(left, right) * slope_two[at, :].astype(f32)
+        upstream = dot(left, weights[2][...].reshape(C_IN, C_MID)) * slope_two[at, :].astype(f32)
         slope_two[at, :] = upstream.astype(bf16)
         count_in(slice(0, C_MID), upstream, hidden_two[at, :].astype(f32))
         hook_in(12, index, 3)
@@ -1299,8 +1360,7 @@
 
     @pl.loop(0, BLOCKS)
     def _(block):
-        three = hidden_three[pl.ds(pl.multiple_of(block * rows, 16), rows), :]
-        grad = dot_rows(act_two[...], three)
+        grad = dot(turned(act_two), hidden_three[pl.ds(pl.multiple_of(block * rows, 16), tall), :])
         weights[2][block] = grad.astype(bf16).reshape(plan.z, plan.x, -1, C_MID)
 
         @pl.when(block == 1)
@@ -1326,22 +1386,27 @@
                 put(pixel, cols, grad.astype(bf16))
             hook_in(site, pixel, SIDE, SIDE - 1, SIDE)
 
-    apply_grad(hidden_two, slope_two, put_padded(padded_two), 14)
+    def put_two(pixel, cols, value):
+        put_padded(padded_two)(pixel, cols, value)
+        slope_two[pl.ds(pl.multiple_of(pixel * views, 16), views), cols] = value
+
+    apply_grad(hidden_two, slope_two, put_two, 14)
+    turn_rows(slope_two)
     column_places = [
         hidden_three.at[pl.ds(2 * rows, rows)],
         hidden_three.at[pl.ds(3 * rows, rows)],
-        hidden_two,
-        slope_two,
+        hidden_two.at[pl.ds(0, rows)],
+        hidden_three.at[pl.ds(2 * rows, rows)],
     ]
     column_loads = [feature_copy(block, column_places[block]) for block in range(BLOCKS)]
-    for copy in column_loads:
+    for copy in column_loads[:3]:
         copy.start()
     def tap_grad(tap):
         down, across = tap // 3, tap % 3
         left = padded_one[pl.ds(down, SIDE), pl.ds(pl.multiple_of(across * views, 16), chunk), :]
-        right = padded_two[1 : SIDE + 1, views : views + chunk, :]
-        grad = dot_rows(left.reshape(rows, C_MID), right.reshape(rows, C_MID))
-        stage_ref[pl.ds(pl.multiple_of(tap * C_MID, 16), C_MID), :] = grad.astype(bf16)
+        right = jnp.concatenate([left.reshape(rows, C_MID), jnp.zeros((tall - rows, C_MID), bf16)], axis=0)
+        grad = dot(turned(slope_two), right).astype(bf16).T
+        stage_ref[pl.ds(pl.multiple_of(tap * C_MID, 16), C_MID), :] = grad
 
     @pl.loop(0, 7)
     def _(tap):
@@ -1349,10 +1414,9 @@
         hook_in(15, tap, 7)
 
     def second_back(first, count):
-        flat = weights[1][...].reshape(9 * C_MID, C_MID)
-        right = jnp.concatenate([flat[tap * C_MID : (tap + 1) * C_MID, :] for tap in range(9)], axis=1)
         at = image_rows(first, count)
-        upstream = dot_cols(patch(padded_two, first, count, True), right) * slope_one[at, :].astype(f32)
+        upstream = dot(patch(padded_two, first, count, True), weights[1][...].reshape(9 * C_MID, C_MID))
+        upstream = upstream * slope_one[at, :].astype(f32)
         slope_one[at, :] = upstream.astype(bf16)
         count_in(slice(0, C_MID), upstream, hidden_one[at, :].astype(f32))
 
@@ -1380,20 +1444,28 @@
     grad_coefs(0, sum_one_back.finish(), row_total)
 
     def put_one(pixel, cols, value):
-        act_two[pl.ds(pl.multiple_of(pixel * views, 16), views), cols] = value
+        put_rows(pixel, cols, value)
+        slope_one[pl.ds(pl.multiple_of(pixel * views, 16), views), cols] = value
 
     apply_grad(hidden_one, slope_one, put_one, 18)
+    turn_rows(slope_one)
 
     def block_grad(block):
-        column_loads[block].wait()
-        grad = dot_rows(column_places[block][...], act_two[...])
-        mem.g1[block] = grad.astype(bf16).reshape(plan.x, -1, C_MID)
-
-    tail = Ring(hidden_three, 2 * rows)
+        if block != 1:
+            column_loads[block].wait()
+        start = 3 * rows if block == 1 else 2 * rows
+        right = hidden_two[...] if block == 2 else hidden_three[start : start + tall, :]
+        grad = dot(turned(slope_one), right).astype(bf16).T
+        mem.g1[block] = grad.reshape(plan.x, -1, C_MID)
+
+    column_loads[1].wait()
+    tail = Ring(hidden_two, 0)
     for block in range(BLOCKS):
         block_grad(block)
+        if block == 0:
+            column_loads[3].start()
         hook(19, block)
-        if block == 1:
+        if block == 2:
             tail.first_loads(slope_hbm)
 
     sum_last = Sum(9)
@@ -1401,14 +1473,13 @@
     @pl.loop(0, pieces)
     def _(index):
         block = index // CHUNKS
-        weight = weights[0][block].reshape(C_MID, C_MID)
-        back = dot_cols(act_two[span(lax.rem(index, CHUNKS)), :], weight)
+        back = dot(act_two[span(lax.rem(index, CHUNKS)), :], weights[0][block].reshape(C_MID, C_MID))
         tail.copy(slope_hbm, index, True).wait()
         cols = pl.ds(pl.multiple_of(block * C_MID, LANES), C_MID)
         for pixel in range(SIDE):
             at = tail.rows(index, pixel, views)
-            summed = hidden_three[at, :].astype(f32) * pool_slope[:, cols]
-            hidden_three[at, :] = (summed + back[pixel * views : (pixel + 1) * views]).astype(bf16)
+            summed = hidden_two[at, :].astype(f32) * pool_slope[:, cols]
+            hidden_two[at, :] = (summed + back[pixel * views : (pixel + 1) * views]).astype(bf16)
         tail.save(outs.features_grad, index)
         tail.next_load(slope_hbm, index)
         hook_in(20, index, pieces)
@@ -1519,11 +1590,11 @@
         stage_sem=dma((2, SLOTS)),
         column_sem=dma((BLOCKS,)),
         h1=pltpu.VMEM((rows, C_MID), bf16),
-        d1=pltpu.VMEM((rows, C_MID), bf16),
-        h2=pltpu.VMEM((rows, C_MID), bf16),
-        d2=pltpu.VMEM((rows, C_MID), bf16),
-        a2=pltpu.VMEM((rows, C_MID), bf16),
-        h3=pltpu.VMEM((BLOCKS * rows, C_MID), bf16),
+        d1=pltpu.VMEM((plan.tall, C_MID), bf16),
+        h2=pltpu.VMEM((plan.tall, C_MID), bf16),
+        d2=pltpu.VMEM((plan.tall, C_MID), bf16),
+        a2=pltpu.VMEM((plan.tall, C_MID), bf16),
+        h3=pltpu.VMEM((3 * rows + plan.tall, C_MID), bf16),
         pad1=pltpu.VMEM((SIDE + 2, (SIDE + 2) * views, C_MID), bf16),
         pad2=pltpu.VMEM((SIDE + 2, (SIDE + 2) * views, C_MID), bf16),
         pool=pltpu.VMEM((views, C_IN), f32),

time: 307 us -> 306 us (level)
  no operation moved by 1% of the time
where the time goes in v3:
time: 306 us; the launch traced here: 305 us
  Pallas kernels  305 us (100%)
    pallas_call x1, Pallas kernels, run_kernel(): pl.pallas_call(lambda *refs: kernel(plan, *refs), out_shape=[jax.ShapeDty...  290 us
    pallas_call x1, Pallas kernels, finish(): pl.pallas_call(lambda *refs: finish_kernel(rates, decays, *refs), grid=(C...  14.6 us

profile of v3, /device:TPU:0, one launch (start us, length us, event | category | flops | bytes accessed | tf_op | source)
XLA Modules:
  0.0 305.5 jit_solution(2719868819174377319)
XLA Ops:
  0.7 290.0 %train_step.1 = (bf16[2352,2048]{1,0:T(8,128)(2,1)}, bf16[2352,2048]{1,0:T(8,128)(2,1)}, f32[2,128]{1,0:T(2,128)}, f32[8,128]{1,0:T(8,128)}, f32[256,128]{1,0:T(...) custom-call(bf16[2352,2048]{1,0:T(8,128)(2,1)} %bitcast.14, ...), custom_call_target="tpu_custom_call" | custom-call | tf_op jit(solution)/shard_map/train_step/pallas_call | solution.py:1625
  290.7 14.6 %finish.1 = (f32[2352,2048]{1,0:T(8,128)}, f32[1,1]{1,0:T(1,128)}, f32[1,1]{1,0:T(1,128)}, f32[256,128]{1,0:T(8,128)}, f32[576,128]{1,0:T(8,128)}, /*index=5*/f3...) custom-call(bf16[2352,2048]{1,0:T(8,128)(2,1)} %get-tuple-element.50, ...), custom_call_target="tpu_custom_call" | custom-call | tf_op jit(solution)/shard_map/finish/pallas_call | solution.py:1705

commit v4 on v3

--- a/solution.py
+++ b/solution.py
@@ -17,7 +17,8 @@
 LANES = 128
 BLOCKS = C_IN // C_MID
 CHUNKS = SIDE
-SLOTS = 6
+SLOTS = 7
+AHEAD = SLOTS - 2
 LAST_SUM = 23
 COPIES = 360
 
@@ -106,14 +107,7 @@
         )
 
     pairs = tuple((matrix, (row_all == col_all).astype(f32)) for matrix in matrices)
-    done = [[] for _ in matrices]
-    size = P_OUT // 4
-    for _ in range(4):
-        pairs = lax.fori_loop(0, size // 8, panel, pairs)
-        for found, (_, right) in zip(done, pairs):
-            found.append(right[-size:])
-        pairs = tuple((left[:-size], right[:-size]) for left, right in pairs)
-    return [jnp.concatenate(found, axis=0) for found in done]
+    return [right for _, right in lax.fori_loop(0, P_OUT // 8, panel, pairs)]
 
 
 def pack_pair(first, second):
@@ -413,6 +407,9 @@
             return 0, 2 * size
         return half * size, size
 
+    def aligned(start, size):
+        return pl.ds(start if isinstance(start, int) else pl.multiple_of(start, 16), size)
+
     def column_span(which, dp_index):
         width = plan.width[which]
         return pl.ds(pl.multiple_of(dp_index * width, width), width)
@@ -433,10 +430,10 @@
         z_one = everything if z_index is None else z_index
         x_one = everything if x_index is None else x_index
         if which == 2:
-            return [(dp_index, z_one, x_one, pl.ds(start, size), everything)]
+            return [(dp_index, z_one, x_one, aligned(start, size), everything)]
         if which == 4:
             return [(z_one, x_one, pl.ds(pl.multiple_of(dp_index * 32 + start, 16), size), everything)]
-        return [(z_one, x_one, pl.ds(start, size), column_span(which, dp_index))]
+        return [(z_one, x_one, aligned(start, size), column_span(which, dp_index))]
 
     recv_parts = {
         1: lambda index: mem.h3.at[index],
@@ -631,20 +628,26 @@
             return self.room(places(self.which, z_from, x_other, dp_far, None)[0])
 
         def add(self, z_index, pairs):
-            def one(z_one):
+            step = min(32, row_span(self.which, pairs[0][0][2])[1])
+
+            def one(z_one, offset):
                 for here, there in pairs:
+                    rows_here = (row_span(self.which, here[2])[0] + offset, step)
+                    rows_there = (row_span(self.which, there[2])[0] + offset, step)
                     for x_step in range(plan.x) if here[0] is None else [None]:
                         x_here = x_step if here[0] is None else here[0]
                         x_there = x_step if there[0] is None else there[0]
-                        index = places(self.which, z_one, x_here, *here[1:])[0]
-                        other = places(self.which, z_one, x_there, *there[1:])[0]
+                        index = places(self.which, z_one, x_here, here[1], rows_here)[0]
+                        other = places(self.which, z_one, x_there, there[1], rows_there)[0]
                         total = self.ref[index].astype(f32) + self.room(other)[...].astype(f32)
                         self.ref[index] = total.astype(bf16)
 
-            if z_index is None:
-                pl.loop(0, plan.z)(one)
-            else:
-                one(z_index)
+            @pl.loop(0, row_span(self.which, pairs[0][0][2])[1] // step)
+            def _(part):
+                if z_index is None:
+                    pl.loop(0, plan.z)(lambda z_one: one(z_one, part * step))
+                else:
+                    one(z_index, part * step)
 
         def core_start(self, place=0):
             if plan.inside:
@@ -833,24 +836,23 @@
             )
 
         def first_loads(self, array):
-            for index in range(3):
+            for index in range(AHEAD):
                 self.copy(array, index, True).start()
 
         def next_load(self, array, index):
-            @pl.when(index + 3 < pieces)
+            @pl.when(index + AHEAD < pieces)
             def _():
-                self.copy(array, index + 3, True).start()
+                self.copy(array, index + AHEAD, True).start()
 
         def save(self, array, index):
             self.copy(array, index, False).start()
 
-            @pl.when(index >= 2)
+            @pl.when(index >= 1)
             def _():
-                self.copy(array, index - 2, False).wait()
+                self.copy(array, index - 1, False).wait()
 
         def last_saves(self, array):
-            for index in (pieces - 2, pieces - 1):
-                self.copy(array, index, False).wait()
+            self.copy(array, pieces - 1, False).wait()
 
     stage_ref = mem.stage
     stage = Ring(stage_ref, 0)
@@ -1023,13 +1025,11 @@
     hidden_one, slope_one = mem.h1, mem.d1
     hidden_two, slope_two = mem.h2, mem.d2
     act_two = mem.a2
-    long = rows // 3
-
     def span(index):
         return pl.ds(pl.multiple_of(index * chunk, 16), chunk)
 
-    def long_rows(block, index):
-        return pl.ds(pl.multiple_of(block * rows + index * long, 16), long)
+    def block_rows(block, index):
+        return pl.ds(pl.multiple_of(block * rows + index * chunk, 16), chunk)
 
     def put_sides(ref, at, sides, hidden):
         for place, cols in enumerate(sides):
@@ -1045,13 +1045,12 @@
     def _(side):
         sides = own_columns(side)
 
-        @pl.loop(0, 3)
+        @pl.loop(0, CHUNKS)
         def _(index):
-            left = jnp.concatenate([hidden_three[long_rows(block, index), :] for block in range(BLOCKS)], axis=1)
+            left = jnp.concatenate([hidden_three[block_rows(block, index), :] for block in range(BLOCKS)], axis=1)
             right = jnp.concatenate([weights[0][:, :, :, cols].reshape(C_IN, LANES) for cols in sides], axis=1)
-            put_sides(hidden_one, long_rows(0, index), sides, dot(left, right))
-
-            hook_in(0, side * 3 + index, 6)
+            put_sides(hidden_one, block_rows(0, index), sides, dot(left, right))
+            hook_in(0, side * CHUNKS + index, 6, 1, 2)
 
         @pl.when(side == 0)
         def _():
@@ -1110,12 +1109,10 @@
     def _(side):
         sides = own_columns(side)
 
-        @pl.loop(0, 3)
+        @pl.loop(0, CHUNKS)
         def _(index):
-            second_part(sides, 2 * index, 2)
-            hook_in(5, side * 4 + index, 8)
-
-        second_part(sides, 6, 1)
+            second_part(sides, index, 1)
+            hook_in(5, side * 8 + index, 8, 1, 2)
 
         @pl.when(side == 0)
         def _():
@@ -1148,12 +1145,12 @@
     def _(block):
         cols = pl.ds(pl.multiple_of(block * C_MID, LANES), C_MID)
 
-        @pl.loop(0, 3)
+        @pl.loop(0, CHUNKS)
         def _(index):
-            hidden = dot(act_two[long_rows(0, index), :], weight_three(block))
-            hidden_three[long_rows(block, index), :] = hidden.astype(bf16)
+            hidden = dot(act_two[block_rows(0, index), :], weight_three(block))
+            hidden_three[block_rows(block, index), :] = hidden.astype(bf16)
             count_in(cols, hidden, hidden)
-            hook_in(9, block * 3 + index, 12)
+            hook_in(9, block * 8 + index, 12, 2, 2)
 
         @pl.when(block == 1)
         def _():
@@ -1212,7 +1209,13 @@
 
     pooled = (pool[...] * (1.0 / PIX)).astype(bf16)
     mem.pooled[...] = pooled
-    proj_hidden = dot(pooled, whole(3))
+
+    @pl.loop(0, P_HID // C_MID)
+    def _(half):
+        cols = pl.ds(pl.multiple_of(half * C_MID, LANES), C_MID)
+        mem.proj_hidden[:, cols] = dot(mem.pooled[...], weights[3][:, :, :, cols].reshape(C_IN, C_MID))
+
+    proj_hidden = mem.proj_hidden[...]
     sum_four = Sum(4)
     sum_four.start(column_sums(proj_hidden), column_sums(proj_hidden * proj_hidden))
     pl.loop(0, 2)(lambda block: turn_weight(3, block))
@@ -1225,7 +1228,6 @@
     proj_act = value.astype(bf16)
     mem.proj_act[...] = proj_act
     mem.proj_slope[...] = slope
-    mem.proj_hidden[...] = proj_hidden
 
     def weight_five(block):
         return weights[4][block // plan.x, block % plan.x]
@@ -1318,8 +1320,12 @@
     plain = row_sums[0:1, :]
     sum_three_back = Sum(6)
     sum_three_back.start(plain, xhat_sum(2, plain, row_sums[1:2, :]))
-    grad_four = dot_rows(mem.pooled[...], four_low).astype(bf16)
-    weights[3][...] = grad_four.reshape(weights[3].shape)
+
+    @pl.loop(0, BLOCKS)
+    def _(block):
+        left = mem.pooled[:, pl.ds(pl.multiple_of(block * C_MID, LANES), C_MID)]
+        weights[3][block] = dot_rows(left, four_low).astype(bf16).reshape(plan.x, -1, P_HID)
+
     sum_three_back.middle()
     hook(23)
     grad_coefs(2, sum_three_back.finish(), row_total)
@@ -1345,14 +1351,14 @@
 
         hook_in(11, index, pieces)
 
-    @pl.loop(0, 3)
+    @pl.loop(0, CHUNKS)
     def _(index):
-        at = long_rows(0, index)
-        left = jnp.concatenate([hidden_three[long_rows(block, index), :] for block in range(BLOCKS)], axis=1)
+        at = block_rows(0, index)
+        left = jnp.concatenate([hidden_three[block_rows(block, index), :] for block in range(BLOCKS)], axis=1)
         upstream = dot(left, weights[2][...].reshape(C_IN, C_MID)) * slope_two[at, :].astype(f32)
         slope_two[at, :] = upstream.astype(bf16)
         count_in(slice(0, C_MID), upstream, hidden_two[at, :].astype(f32))
-        hook_in(12, index, 3)
+        hook_in(12, index, 3, 2, 2)
 
     sums = row_sums[0:1, :C_MID], row_sums[1:2, :C_MID]
     sum_two_back = Sum(7)
@@ -1392,15 +1398,16 @@
 
     apply_grad(hidden_two, slope_two, put_two, 14)
     turn_rows(slope_two)
-    column_places = [
-        hidden_three.at[pl.ds(2 * rows, rows)],
-        hidden_three.at[pl.ds(3 * rows, rows)],
-        hidden_two.at[pl.ds(0, rows)],
-        hidden_three.at[pl.ds(2 * rows, rows)],
-    ]
-    column_loads = [feature_copy(block, column_places[block]) for block in range(BLOCKS)]
-    for copy in column_loads[:3]:
-        copy.start()
+    def column_copy(block):
+        return pltpu.make_async_copy(
+            features.at[:, pl.ds(pl.multiple_of(block * C_MID, LANES), C_MID)],
+            hidden_three.at[pl.ds(pl.multiple_of((2 + block % 2) * rows, 16), rows)],
+            mem.column_sem.at[block],
+        )
+
+    column_copy(0).start()
+    column_copy(1).start()
+
     def tap_grad(tap):
         down, across = tap // 3, tap % 3
         left = padded_one[pl.ds(down, SIDE), pl.ds(pl.multiple_of(across * views, 16), chunk), :]
@@ -1420,12 +1427,11 @@
         slope_one[at, :] = upstream.astype(bf16)
         count_in(slice(0, C_MID), upstream, hidden_one[at, :].astype(f32))
 
-    @pl.loop(0, 3)
+    @pl.loop(0, CHUNKS)
     def _(index):
-        second_back(2 * index, 2)
-        hook_in(16, index, 3)
-
-    second_back(6, 1)
+        second_back(index, 1)
+        hook_in(16, index, 3, 1, 2)
+
     hook(16, 3)
     sums = row_sums[0:1, :C_MID], row_sums[1:2, :C_MID]
     sum_one_back = Sum(8)
@@ -1450,23 +1456,22 @@
     apply_grad(hidden_one, slope_one, put_one, 18)
     turn_rows(slope_one)
 
-    def block_grad(block):
-        if block != 1:
-            column_loads[block].wait()
-        start = 3 * rows if block == 1 else 2 * rows
-        right = hidden_two[...] if block == 2 else hidden_three[start : start + tall, :]
+    tail = Ring(hidden_two, 0)
+    tail.first_loads(slope_hbm)
+
+    @pl.loop(0, BLOCKS)
+    def _(block):
+        column_copy(block).wait()
+        found = hidden_three[pl.ds(pl.multiple_of((2 + block % 2) * rows, 16), rows), :]
+        right = jnp.concatenate([found, jnp.zeros((tall - rows, C_MID), bf16)], axis=0)
         grad = dot(turned(slope_one), right).astype(bf16).T
         mem.g1[block] = grad.reshape(plan.x, -1, C_MID)
 
-    column_loads[1].wait()
-    tail = Ring(hidden_two, 0)
-    for block in range(BLOCKS):
-        block_grad(block)
-        if block == 0:
-            column_loads[3].start()
-        hook(19, block)
-        if block == 2:
-            tail.first_loads(slope_hbm)
+        @pl.when(block + 2 < BLOCKS)
+        def _():
+            column_copy(block + 2).start()
+
+        hook_in(19, block, BLOCKS)
 
     sum_last = Sum(9)
 
@@ -1661,7 +1666,12 @@
     refs = refs[2:]
     given, wide, loss, norm, updated = refs[: 4 * count], *refs[4 * count : 4 * count + 3], refs[4 * count + 3 : -2]
     rooms, sems = refs[-2], refs[-1]
-    wide[...] = low[...].astype(f32)
+
+    @pl.loop(0, low.shape[0] // 16)
+    def _(part):
+        at = pl.ds(pl.multiple_of(part * 16, 16), 16)
+        wide[at, :] = low[at, :].astype(f32)
+
     step = pl.program_id(0)
 
     def load(place):
@@ -1682,10 +1692,17 @@
         for place in range(4 * count):
             load(place).wait()
         for place in range(count):
-            weight, first, second, grad = (rooms[part * count + place][...] for part in range(4))
-            found = adam_update(weight, first, second, grad * scalars[3, 0], rates[place], decays[place])
-            for part in range(3):
-                rooms[part * count + place][...] = found[part]
+            rows = rooms[place].shape[0]
+            tile = 16 if rows % 16 == 0 else rows
+
+            @pl.loop(0, rows // tile)
+            def _(index, place=place, tile=tile):
+                at = pl.ds(pl.multiple_of(index * tile, tile), tile)
+                weight, first, second, grad = (rooms[part * count + place][at, :] for part in range(4))
+                found = adam_update(weight, first, second, grad * scalars[3, 0], rates[place], decays[place])
+                for part in range(3):
+                    rooms[part * count + place][at, :] = found[part]
+
         for place in range(3 * count):
             store(place).start()
 

time: 306 us -> 318 us (1.039)
  Pallas kernels: 305 us -> 317 us
    pallas_call x1, Pallas kernels: 290 us -> 300 us  [run_kernel(): pl.pallas_call(lambda *refs: kernel(plan, *refs), out_shape=[jax.ShapeDty...]
where the time goes in v4:
time: 318 us
  Pallas kernels  317 us (100%)
    pallas_call x1, Pallas kernels, run_kernel(): pl.pallas_call(lambda *refs: kernel(plan, *refs), out_shape=[jax.ShapeDty...  300 us
    pallas_call x1, Pallas kernels, finish(): pl.pallas_call(lambda *refs: finish_kernel(rates, decays, *refs), grid=(C...  16.6 us

profile of v4, /device:TPU:0, one launch (start us, length us, event | category | flops | bytes accessed | tf_op | source)
XLA Modules:
  0.0 317.6 jit_solution(9662782755492592021)
XLA Ops:
  0.7 300.2 %train_step.1 = (bf16[2352,2048]{1,0:T(8,128)(2,1)}, bf16[2352,2048]{1,0:T(8,128)(2,1)}, f32[2,128]{1,0:T(2,128)}, f32[8,128]{1,0:T(8,128)}, f32[256,128]{1,0:T(...) custom-call(bf16[2352,2048]{1,0:T(8,128)(2,1)} %bitcast.14, ...), custom_call_target="tpu_custom_call" | custom-call | tf_op jit(solution)/shard_map/train_step/pallas_call | solution.py:1630
  300.9 16.6 %finish.1 = (f32[2352,2048]{1,0:T(8,128)}, f32[1,1]{1,0:T(1,128)}, f32[1,1]{1,0:T(1,128)}, f32[256,128]{1,0:T(8,128)}, f32[576,128]{1,0:T(8,128)}, /*index=5*/f3...) custom-call(bf16[2352,2048]{1,0:T(8,128)(2,1)} %get-tuple-element.50, ...), custom_call_target="tpu_custom_call" | custom-call | tf_op jit(solution)/shard_map/finish/pallas_call | solution.py:1722
